TPU v7x, 256 devices: a whole 4x4x8 slice. The times are simulated.
256 devices in a mesh: dp: 32 (over z, y), tensor: 8 (over x, core).
Axes of the slice: x: 4, y: 4, z: 8, core: 2. Of those that a mesh axis runs over, the one named last changes fastest.
Arguments:
- grad_a_parts: bfloat16 [32, 32, 5120, 64], P('dp', None, 'tensor'), may hold values from -6 to 6
- grad_b_parts: bfloat16 [32, 32, 64, 8192], P('dp', None, None, 'tensor'), may hold values from -6 to 6
- adapter_a: float32 [32, 5120, 64], P('dp', 'tensor'), may hold values from -0.078125 to 0.078125
- adapter_b: float32 [32, 64, 8192], P('dp', None, 'tensor'), may hold values from -0.75 to 0.75
- moment_a: float32 [32, 5120, 64], P('dp', 'tensor'), may hold values from -8 to 8
- moment_b: float32 [32, 64, 8192], P('dp', None, 'tensor'), may hold values from -8 to 8
- second_a: float32 [32, 5120, 64], P('dp', 'tensor'), may hold values from 0.001 to 0.1
- second_b: float32 [32, 64, 8192], P('dp', None, 'tensor'), may hold values from 0.001 to 0.1
- group_policy: int32 [32, 16], replicated, may hold values from 0 to 31, as said below
- row_slot: int32 [4096], P('dp'), may hold values from 0 to 15, as said below
- cache_length: int32 [4096], P('dp'), may hold values from 1 to 48, as said below
- features: bfloat16 [4096, 5120], P('dp', 'tensor'), may hold values from -6 to 6
- frozen_query_output: bfloat16 [4096, 8192], P('dp', 'tensor'), may hold values from -80 to 80
- kv_cache: bfloat16 [2, 4096, 8, 48, 128], P(None, 'dp', 'tensor'), may hold values from -4 to 4
- new_kv: bfloat16 [2, 4096, 8, 128], P(None, 'dp', 'tensor'), may hold values from -4 to 4
Outputs:
- new_a: float32 [32, 5120, 64], P('dp', 'tensor')
- new_b: float32 [32, 64, 8192], P('dp', None, 'tensor')
- new_moment_a: float32 [32, 5120, 64], P('dp', 'tensor')
- new_moment_b: float32 [32, 64, 8192], P('dp', None, 'tensor')
- new_second_a: float32 [32, 5120, 64], P('dp', 'tensor')
- new_second_b: float32 [32, 64, 8192], P('dp', None, 'tensor')
- attended: bfloat16 [4096, 8192], P('dp', 'tensor')
Inputs may be any that keep to these rules, and one draw needn't show every extreme that they name: Each row of group_policy holds 16 different policies in rising order. `row_slot`: within each group of 128 rows the slots never fall; every group's first row has slot 0 and its last row slot 15; no slot of a group is used by more than 16 rows, and slot 0 of every group by exactly 16. `cache_length`: the first row of every group of 128 rows holds 48 positions and its second row one.
All inputs are finite; a program needn't handle non-finite values.
Results may differ from a plain program's by a relative error of at most 0.025.
Values may be sent and summed in bfloat16 or wider, within the bound.
No kernel may reach another device: no remote copies, remote signals or barrier semaphores. Data moves between devices by JAX's collectives and lax.ppermute only.
A program may use at most 128 MiB of HBM per device.

v0:
```python
import math

import jax
import jax.numpy as jnp
from jax import lax
from jax.experimental import pallas as pl
from jax.experimental.pallas import tpu as pltpu
from jax.sharding import Mesh
from jax.sharding import PartitionSpec as P

BETA_ONE = 0.9
BETA_TWO = 0.999
LEARN_RATE = 0.001
EPSILON = 1e-08
WEIGHT_SHRINKAGE = 0.01
LOWRANK_SCALE = 2.0
FIRST_FIX = 1.0 - 0.9**10
SECOND_FIX = 1.0 - 0.999**10
NZ, NY, NX, NC = 8, 4, 4, 2
SIZES = {"z": NZ, "y": NY, "x": NX, "c": NC}
F32 = jnp.float32
BF16 = jnp.bfloat16
CAP = 16
PIECES = 2


def adamw(param, moment, second, gradient):
    new_moment = BETA_ONE * moment + (1.0 - BETA_ONE) * gradient
    new_second = BETA_TWO * second + (1.0 - BETA_TWO) * gradient * gradient
    stepped = new_moment / FIRST_FIX / (jnp.sqrt(new_second / SECOND_FIX) + EPSILON)
    return (param - LEARN_RATE * (stepped + WEIGHT_SHRINKAGE * param), new_moment, new_second)


def shift(value, axis, by):
    size = SIZES[axis]
    return lax.ppermute(value, axis, [(i, (i + by) % size) for i in range(size)])


def crossed(value, by, flip):
    pairs = [(2 * x + c, 2 * ((x + by) % NX) + (c ^ flip)) for x in range(NX) for c in range(NC)]
    return lax.ppermute(value, ("x", "c"), pairs)


def tied(*values):
    return lax.optimization_barrier(values)


def after(values, *done):
    return lax.optimization_barrier((*values, *done))[: len(values)]


class Ring:
    def __init__(self, parts, axis, dim):
        self.parts, self.axis, self.dim = parts, axis, dim
        self.size, self.me = SIZES[axis], lax.axis_index(axis)
        self.left = self.size // 2

    def chunk(self, offset):
        place = lax.rem(self.me + (offset + self.size), self.size)
        return lax.dynamic_index_in_dim(self.parts, place, self.dim, keepdims=False)

    def send(self, up, down):
        up, down = tied(up, down)
        return tied(shift(up, self.axis, 1), shift(down, self.axis, -1))

    def first(self):
        chunk = self.chunk(self.left)
        self.half = chunk.shape[0] // 2
        return chunk[self.half :], chunk[: self.half]

    def step(self, up, down):
        up, down = up.astype(F32), down.astype(F32)
        if 2 * self.left == self.size:
            spare = [(0, 0, 0)] * (up.ndim - 1)
            zero = jnp.zeros((), F32)
            up = lax.pad(up, zero, [(self.half, 0, 0)] + spare)
            down = lax.pad(down, zero, [(0, self.half, 0)] + spare)
        self.left -= 1
        up = (self.chunk(self.left).astype(F32) + up).astype(BF16)
        down = (self.chunk(-self.left).astype(F32) + down).astype(BF16)
        return up, down

    def total(self, up, down):
        return (self.chunk(0).astype(F32) + up.astype(F32) + down.astype(F32)).astype(BF16)


def swapped_sum(parts, axis):
    parts = lax.all_to_all(parts, axis, 0, 0)
    terms = [parts[i].astype(F32) for i in range(SIZES[axis])]
    while len(terms) > 1:
        terms = [left + right for left, right in zip(terms[::2], terms[1::2])]
    return terms[0]


def sent_sum(parts, axis):
    size = SIZES[axis]
    me = lax.axis_index(axis)

    def chunk(offset):
        return lax.dynamic_index_in_dim(parts, lax.rem(me + offset, size), 0, keepdims=False)

    sent = tied(*[chunk(offset) for offset in range(1, size)])
    came = tied(*[shift(part, axis, 1 + i) for i, part in enumerate(sent)])
    total = chunk(0).astype(F32)
    for part in came:
        total = total + part.astype(F32)
    return total, sent


def tensor_sum(value):
    core = lax.axis_index("c")
    both = (value + shift(value, "c", 1)).reshape(2, value.shape[0] // 2, value.shape[1])
    mine = lax.dynamic_index_in_dim(both, core, 0, keepdims=False)
    other = lax.dynamic_index_in_dim(both, 1 - core, 0, keepdims=False)
    mine, other = tied(mine, other)
    one, two, three = tied(crossed(other, 1, 1), crossed(mine, NX - 1, 0), crossed(mine, 2, 0))
    total = ((mine + one) + (two + three)).astype(BF16)
    other = shift(total, "c", 1)
    return jnp.where(
        core == 0, jnp.concatenate([total, other], axis=0), jnp.concatenate([other, total], axis=0)
    )


def decode_kernel(place_ref, length_ref, delta_ref, frozen_ref, cache_hbm, new_ref, out_ref, query, cache_ref, arrived):
    block = out_ref.shape[0] // PIECES
    copies = []
    for piece in range(PIECES):
        part = (slice(None), slice(piece * block, (piece + 1) * block))
        copies.append(pltpu.make_async_copy(cache_hbm.at[part], cache_ref.at[part], arrived.at[piece]))
        copies[-1].start()
    total, spots = query.shape[0], delta_ref.shape[0]
    pick = lax.broadcasted_iota(jnp.int32, (total, spots), 1) == place_ref[...]
    pick = jnp.where(pick, 1.0, 0.0).astype(BF16)
    mine = jnp.dot(pick, delta_ref[...], preferred_element_type=F32)
    vector = frozen_ref[...].astype(F32) + LOWRANK_SCALE * mine
    query[...] = vector.astype(BF16).astype(F32)
    for piece in range(PIECES):
        copies[piece].wait()
        decode_rows(piece * block, block, length_ref, cache_ref, new_ref, out_ref, query)


def decode_rows(base, block, length_ref, cache_ref, new_ref, out_ref, query):
    span, width = cache_ref.shape[3], cache_ref.shape[4]
    heads = out_ref.shape[1] // width
    inverse = 1.0 / math.sqrt(width)
    column = lax.broadcasted_iota(jnp.int32, (8, 8 * span), 1)
    first = lax.broadcasted_iota(jnp.int32, (8, 8 * span), 0) * span
    starts = range(base, base + block, 8)
    stack = lambda value: jnp.concatenate([value] * heads, axis=0)
    rows, scores, valid = [], [], []
    for low in starts:
        piece = query[low : low + 8, :]
        piece = jnp.concatenate([piece[:, h * width : (h + 1) * width] for h in range(heads)], axis=0)
        keys = cache_ref[0, low : low + 8, 0].reshape(8 * span, width)
        rows.append(piece)
        scores.append(
            lax.dot_general(piece.astype(BF16), keys, (((1,), (1,)), ((), ())), preferred_element_type=F32)
        )
    probs, own_probs = [], []
    for i, low in enumerate(starts):
        length = length_ref[low : low + 8, :]
        valid = (column >= first) & (column < first + length)
        bias = stack(jnp.where(valid, 0.0, -1e30))
        score = scores[i] * inverse + bias
        own = jnp.sum(rows[i] * stack(new_ref[0, low : low + 8, :].astype(F32)), axis=1, keepdims=True) * inverse
        peak = jnp.maximum(jnp.max(score, axis=1, keepdims=True), own)
        weights = jnp.exp(score - peak)
        own_weight = jnp.exp(own - peak)
        scale = 1.0 / (jnp.sum(weights, axis=1, keepdims=True) + own_weight)
        probs.append((weights * scale).astype(BF16))
        own_probs.append((own_weight * scale).astype(BF16).astype(F32))
    mixed = []
    for i, low in enumerate(starts):
        values = cache_ref[1, low : low + 8, 0].reshape(8 * span, width)
        new_value = stack(new_ref[1, low : low + 8, :].astype(F32))
        mixed.append(jnp.dot(probs[i], values, preferred_element_type=F32) + own_probs[i] * new_value)
    for h in range(heads):
        part = jnp.concatenate([value[8 * h : 8 * h + 8] for value in mixed], axis=0)
        out_ref[base : base + block, h * width : (h + 1) * width] = part.astype(BF16)


def decode(place, length, delta, frozen, kv_cache, new_kv):
    vmem = pl.BlockSpec(memory_space=pltpu.VMEM)
    return pl.pallas_call(
        decode_kernel,
        in_specs=[vmem] * 4 + [pl.BlockSpec(memory_space=pltpu.HBM), vmem],
        out_specs=vmem,
        out_shape=jax.ShapeDtypeStruct(frozen.shape, BF16),
        scratch_shapes=[
            pltpu.VMEM(frozen.shape, F32),
            pltpu.VMEM(kv_cache.shape, BF16),
            pltpu.SemaphoreType.DMA((PIECES,)),
        ],
        compiler_params=pltpu.CompilerParams(vmem_limit_bytes=32 * 1024 * 1024),
    )(place[:, None], length[:, None], delta, frozen, kv_cache, new_kv[:, :, 0])


def shards(
    grad_a_parts,
    grad_b_parts,
    adapter_a,
    adapter_b,
    moment_a,
    moment_b,
    second_a,
    second_b,
    group_policy,
    row_slot,
    cache_length,
    features,
    frozen_query_output,
    kv_cache,
    new_kv,
):
    z, y = lax.axis_index("z"), lax.axis_index("y")
    rows, width = features.shape
    rank = grad_b_parts.shape[2]
    policies = group_policy.shape[0]
    flip = lambda value: jnp.swapaxes(value, -1, -2)

    ring_a = Ring(flip(grad_a_parts[0]).reshape(NZ, NY, rank, width), "z", 0)
    ring_b = Ring(grad_b_parts[0].reshape(NZ, NY, rank, grad_b_parts.shape[3]), "y", 1)
    go_a = ring_a.first()
    go_b = after(ring_b.first(), *go_a)
    come_a, come_b = ring_a.send(*go_a), ring_b.send(*go_b)
    (row_slot,) = after((row_slot,), *go_b)

    my_policies = lax.dynamic_index_in_dim(group_policy, z * NY + y, 0, keepdims=False)
    slot_onehot = row_slot[:, None] == jnp.arange(my_policies.shape[0])[None, :]
    row_policy = jnp.sum(jnp.where(slot_onehot, my_policies[None, :], 0), axis=1)
    before = jnp.sum((row_slot[None, :] < row_slot[:, None]).astype(jnp.int32), axis=1)
    place = row_policy * CAP + jnp.arange(rows, dtype=jnp.int32) - before
    select = (jnp.arange(policies * CAP, dtype=jnp.int32)[:, None] == place[None, :]).astype(BF16)

    packed = jnp.dot(select, features, preferred_element_type=F32).astype(BF16)

    come_a = after(come_a, packed)
    go_a = ring_a.step(*come_a)
    come_a = ring_a.send(*go_a)
    (packed,) = after((packed,), *go_a)
    feats = lax.all_to_all(packed.reshape(policies, CAP, width), ("z", "y"), 0, 0)
    go_b = ring_b.step(*after(come_b, packed))
    come_b = ring_b.send(*go_b)
    go_a = ring_a.step(*after(come_a, *go_b))
    come_a = ring_a.send(*go_a)
    *come_a, feats = tied(*come_a, feats)
    go_a = ring_a.step(*come_a)
    come_a = ring_a.send(*go_a)
    sum_b = ring_b.total(*after(come_b, *go_a))
    grad_b = swapped_sum(sum_b, "z")
    grad_a, _ = sent_sum(ring_a.total(*after(come_a, sum_b)), "y")
    feats = feats.reshape(policies * CAP, width)

    new_a, new_moment_a, new_second_a = adamw(
        flip(adapter_a[0]), flip(moment_a[0]), flip(second_a[0]), grad_a
    )
    partial = lax.dot_general(
        new_a.astype(BF16), feats, (((1,), (1,)), ((), ())), preferred_element_type=F32
    )
    shrink = tensor_sum(partial)

    new_b, new_moment_b, new_second_b = adamw(adapter_b[0], moment_b[0], second_b[0], grad_b)
    delta = lax.dot_general(
        shrink, new_b.astype(BF16), (((0,), (0,)), ((), ())), preferred_element_type=F32
    ).astype(BF16)
    delta = lax.all_to_all(delta.reshape(policies, CAP, -1), ("z", "y"), 0, 0)
    delta = delta.reshape(policies * CAP, -1)
    attended = decode(place, cache_length, delta, frozen_query_output, kv_cache, new_kv)
    return (
        flip(new_a)[None],
        new_b[None],
        flip(new_moment_a)[None],
        new_moment_b[None],
        flip(new_second_a)[None],
        new_second_b[None],
        attended,
    )


def solution(mesh):
    fine = Mesh(mesh.devices.reshape(NZ, NY, NX, NC), ("z", "y", "x", "c"))
    dp, tensor = ("z", "y"), ("x", "c")
    adapter_a, adapter_b = P(dp, tensor, None), P(dp, None, tensor)
    return jax.shard_map(
        shards,
        mesh=fine,
        in_specs=(
            P(dp, None, tensor, None),
            P(dp, None, None, tensor),
            adapter_a,
            adapter_b,
            adapter_a,
            adapter_b,
            adapter_a,
            adapter_b,
            P(),
            P(dp),
            P(dp),
            P(dp, tensor),
            P(dp, tensor),
            P(None, dp, tensor, None, None),
            P(None, dp, tensor, None),
        ),
        out_specs=(adapter_a, adapter_b, adapter_a, adapter_b, adapter_a, adapter_b, P(dp, tensor)),
        check_vma=False,
    )
```

profile of v0, /device:TPU:8, one launch (start us, length us, event | category | flops | bytes accessed | tf_op | source)
XLA Modules:
  0.0 142.8 jit_solution(4769128619453983082)
XLA Ops:
  1.9 2.0 %collective-permute-start = (bf16[2,64,640]{2,1,0:T(8,128)(2,1)S(1)}, bf16[2,64,640]{2,1,0:T(8,128)(2,1)S(1)}, u32[]{:S(2)}, u32[]{:S(2)}) collective-permute-start(bf16[2,64,640]{2,1,0:T(8,128)(2,1)S(1)} %get-tuple-element.59), channel_id=1, source_target_pairs={{0,32},{32,64},{64,96},{96,128},{128,160},{160,192},{192,224},{224... | collective-permute-start | bytes 491528 | tf_op jit(solution)/shard_map/ppermute | solution.py:36
  3.9 4.0 %collective-permute-start.1 = (bf16[2,64,640]{2,1,0:T(8,128)(2,1)S(1)}, bf16[2,64,640]{2,1,0:T(8,128)(2,1)S(1)}, u32[]{:S(2)}, u32[]{:S(2)}) collective-permute-start(bf16[2,64,640]{2,1,0:T(8,128)(2,1)S(1)} %get-tuple-element.60), channel_id=1, source_target_pairs={{0,224},{32,0},{64,32},{96,64},{128,96},{160,128},{192,160},{224,1... | collective-permute-start | bytes 491528 | tf_op jit(solution)/shard_map/ppermute | solution.py:36
  7.9 2.3 %dynamic-slice_bitcast_fusion = (bf16[4,64,1024]{2,1,0:T(8,128)(2,1)}, bf16[4,64,1024]{2,1,0:T(8,128)(2,1)}) fusion(bf16[8,4,64,1024]{3,2,1,0:T(8,128)(2,1)} %bitcast.151, s32[]{:T(128)S(6)} %select_n.77, s32[]{:T(128)S(6)} %add.364), kind=kLoop, calls=%fused_computation.24 | loop fusion | bytes 2097160 | tf_op jit(solution)/shard_map/slice | solution.py:69
  10.2 1.6 %collective-permute-start.4 = (bf16[4,64,1024]{2,1,0:T(8,128)(2,1)}, bf16[4,64,1024]{2,1,0:T(8,128)(2,1)}, u32[]{:S(2)}, u32[]{:S(2)}) collective-permute-start(bf16[4,64,1024]{2,1,0:T(8,128)(2,1)} %get-tuple-element.72), channel_id=1, source_target_pairs={{0,8},{8,16},{16,24},{24,0},{1,9},{9,17},{17,25},{25,1},{2,10},{10... | collective-permute-start | bytes 1572872 | tf_op jit(solution)/shard_map/ppermute | solution.py:36
  14.8 9.0 %all-to-all-start = ((bf16[32,16,640]{2,1,0:T(8,128)(2,1)}), bf16[32,16,640]{2,1,0:T(8,128)(2,1)S(1)}, u32[]{:S(2)}, u32[]{:S(2)}) async-start(bf16[32,16,640]{2,1,0:T(8,128)(2,1)} %bitcast.160), calls=%async_computation | async-start | bytes 1310720 | tf_op jit(solution)/shard_map/all_to_all | solution.py:241
  23.8 1.5 %collective-permute-start.2 = (bf16[4,64,640]{2,1,0:T(8,128)(2,1)}, bf16[4,64,640]{2,1,0:T(8,128)(2,1)}, u32[]{:S(2)}, u32[]{:S(2)}) collective-permute-start(bf16[4,64,640]{2,1,0:T(8,128)(2,1)} %get-tuple-element.68), channel_id=1, source_target_pairs={{0,32},{32,64},{64,96},{96,128},{128,160},{160,192},{192,224},{224... | collective-permute-start | bytes 983048 | tf_op jit(solution)/shard_map/ppermute | solution.py:36
  25.4 1.8 %collective-permute-start.3 = (bf16[4,64,640]{2,1,0:T(8,128)(2,1)}, bf16[4,64,640]{2,1,0:T(8,128)(2,1)}, u32[]{:S(2)}, u32[]{:S(2)}) collective-permute-start(bf16[4,64,640]{2,1,0:T(8,128)(2,1)} %get-tuple-element.69), channel_id=1, source_target_pairs={{0,224},{32,0},{64,32},{96,64},{128,96},{160,128},{192,160},{224,1... | collective-permute-start | bytes 983048 | tf_op jit(solution)/shard_map/ppermute | solution.py:36
  27.1 3.7 %fusion.2 = (bf16[8,64,1024]{2,1,0:T(8,128)(2,1)}, bf16[8,64,1024]{2,1,0:T(8,128)(2,1)}) fusion(bf16[4,64,1024]{2,1,0:T(8,128)(2,1)} %collective-permute-done.5, bf16[8,4,64,1024]{3,2,1,0:T(8,128)(2,1)} %bitcast.152, s32[]{:T(128)S(6)} %select_n.82, bf16[4,64,1024]{2,1,0:T(8,128)(2,1)} %collective-permute-done.4, s32[]{:T(128)S(6)} %select_n.81), kind=kLoop, calls=%fused_computation.4 | loop fusion | flops 4194304 | bytes 5242888 | tf_op jit(solution)/shard_map/convert_element_type | solution.py:80
  30.9 1.5 %collective-permute-start.10 = (bf16[8,64,1024]{2,1,0:T(8,128)(2,1)}, bf16[8,64,1024]{2,1,0:T(8,128)(2,1)}, u32[]{:S(2)}, u32[]{:S(2)}) collective-permute-start(bf16[8,64,1024]{2,1,0:T(8,128)(2,1)} %get-tuple-element.91), channel_id=1, source_target_pairs={{0,8},{8,16},{16,24},{24,0},{1,9},{9,17},{17,25},{25,1},{2,10},{10... | collective-permute-start | bytes 3145736 | tf_op jit(solution)/shard_map/ppermute | solution.py:36
  32.9 13.9 %collective-permute-done.2 = bf16[4,64,640]{2,1,0:T(8,128)(2,1)} collective-permute-done((bf16[4,64,640]{2,1,0:T(8,128)(2,1)}, bf16[4,64,640]{2,1,0:T(8,128)(2,1)}, u32[]{:S(2)}, u32[]{:S(2)}) %collective-permute-start.2) | collective-permute-done | bytes 327712 | tf_op jit(solution)/shard_map/ppermute | solution.py:36
  46.8 2.1 %fusion.5 = (bf16[4,64,640]{2,1,0:T(8,128)(2,1)}, bf16[4,64,640]{2,1,0:T(8,128)(2,1)}) fusion(bf16[4,64,640]{2,1,0:T(8,128)(2,1)} %collective-permute-done.3, bf16[8,4,64,640]{3,2,1,0:T(8,128)(2,1)S(1)} %bitcast.157, s32[]{:T(128)S(6)} %select_n.83, bf16[4,64,640]{2,1,0:T(8,128)(2,1)} %collective-permute-done.2, s32[]{:T(128)S(6)} %select_n.74), kind=kLoop, calls=%fused_computation.12 | loop fusion | flops 1310720 | bytes 1966088 | tf_op jit(solution)/shard_map/convert_element_type | solution.py:80
  49.1 3.1 %collective-permute-start.7 = (bf16[4,64,640]{2,1,0:T(8,128)(2,1)}, bf16[4,64,640]{2,1,0:T(8,128)(2,1)}, u32[]{:S(2)}, u32[]{:S(2)}) collective-permute-start(bf16[4,64,640]{2,1,0:T(8,128)(2,1)} %get-tuple-element.82), channel_id=1, source_target_pairs={{0,224},{32,0},{64,32},{96,64},{128,96},{160,128},{192,160},{224,1... | collective-permute-start | bytes 983048 | tf_op jit(solution)/shard_map/ppermute | solution.py:36
  52.1 6.5 %collective-permute-done.6 = bf16[4,64,640]{2,1,0:T(8,128)(2,1)} collective-permute-done((bf16[4,64,640]{2,1,0:T(8,128)(2,1)}, bf16[4,64,640]{2,1,0:T(8,128)(2,1)}, u32[]{:S(2)}, u32[]{:S(2)}) %collective-permute-start.6) | collective-permute-done | bytes 327712 | tf_op jit(solution)/shard_map/ppermute | solution.py:36
  58.7 2.1 %fusion.4 = (bf16[4,64,640]{2,1,0:T(8,128)(2,1)}, bf16[4,64,640]{2,1,0:T(8,128)(2,1)}) fusion(bf16[4,64,640]{2,1,0:T(8,128)(2,1)} %collective-permute-done.7, bf16[8,4,64,640]{3,2,1,0:T(8,128)(2,1)S(1)} %bitcast.158, s32[]{:T(128)S(6)} %select_n.84, bf16[4,64,640]{2,1,0:T(8,128)(2,1)} %collective-permute-done.6, s32[]{:T(128)S(6)} %select_n.73), kind=kLoop, calls=%fused_computation.10 | loop fusion | flops 1310720 | bytes 1966088 | tf_op jit(solution)/shard_map/convert_element_type | solution.py:80
  62.0 1.9 %collective-permute-start.9 = (bf16[4,64,640]{2,1,0:T(8,128)(2,1)}, bf16[4,64,640]{2,1,0:T(8,128)(2,1)S(1)}, u32[]{:S(2)}, u32[]{:S(2)}) collective-permute-start(bf16[4,64,640]{2,1,0:T(8,128)(2,1)} %get-tuple-element.88), channel_id=1, source_target_pairs={{0,224},{32,0},{64,32},{96,64},{128,96},{160,128},{192,160},{224,1... | collective-permute-start | bytes 983048 | tf_op jit(solution)/shard_map/ppermute | solution.py:36
  64.0 3.5 %fusion.1 = bf16[8,64,1024]{2,1,0:T(8,128)(2,1)} fusion(bf16[8,64,1024]{2,1,0:T(8,128)(2,1)} %collective-permute-done.11, bf16[8,64,1024]{2,1,0:T(8,128)(2,1)} %collective-permute-done.10, bf16[8,4,64,1024]{3,2,1,0:T(8,128)(2,1)} %bitcast.153, s32[]{:T(128)S(6)} %select_n.85), kind=kLoop, calls=%fused_computation.2 | loop fusion | flops 3145728 | bytes 4194308 | tf_op jit(solution)/shard_map/convert_element_type | solution.py:84
  67.5 4.9 %all-to-all-start.1 = ((bf16[8,64,1024]{2,1,0:T(8,128)(2,1)}), bf16[8,64,1024]{2,1,0:T(8,128)(2,1)S(1)}, u32[]{:S(2)}, u32[]{:S(2)}) async-start(bf16[8,64,1024]{2,1,0:T(8,128)(2,1)} %fusion.1), calls=%async_computation.1 | async-start | bytes 2097152 | tf_op jit(solution)/shard_map/all_to_all | solution.py:88
  73.6 1.8 %collective-permute-start.12 = (bf16[64,640]{1,0:T(8,128)(2,1)S(1)}, bf16[64,640]{1,0:T(8,128)(2,1)S(1)}, u32[]{:S(2)}, u32[]{:S(2)}) collective-permute-start(bf16[64,640]{1,0:T(8,128)(2,1)S(1)} %get-tuple-element.99), channel_id=1, source_target_pairs={{0,8},{8,16},{16,24},{24,0},{1,9},{9,17},{17,25},{25,1},{2,10},{10... | collective-permute-start | bytes 245768 | tf_op jit(solution)/shard_map/ppermute | solution.py:36
  76.3 2.0 %collective-permute-start.14 = (bf16[64,640]{1,0:T(8,128)(2,1)S(1)}, bf16[64,640]{1,0:T(8,128)(2,1)}, u32[]{:S(2)}, u32[]{:S(2)}) collective-permute-start(bf16[64,640]{1,0:T(8,128)(2,1)S(1)} %get-tuple-element.101), channel_id=1, source_target_pairs={{0,24},{8,0},{16,8},{24,16},{1,25},{9,1},{17,9},{25,17},{2,26},{10... | collective-permute-start | bytes 245768 | tf_op jit(solution)/shard_map/ppermute | solution.py:36
  78.3 3.3 %collective-permute-done.13 = bf16[64,640]{1,0:T(8,128)(2,1)} collective-permute-done((bf16[64,640]{1,0:T(8,128)(2,1)S(1)}, bf16[64,640]{1,0:T(8,128)(2,1)}, u32[]{:S(2)}, u32[]{:S(2)}) %collective-permute-start.13) | collective-permute-done | bytes 81952 | tf_op jit(solution)/shard_map/ppermute | solution.py:36
  81.7 1.7 %fusion.46 = (f32[1,640,64]{1,2,0:T(8,128)}, f32[64,640]{1,0:T(8,128)S(1)}) fusion(f32[1,640,64]{1,2,0:T(8,128)S(1)} %copy-done.5, bf16[64,640]{1,0:T(8,128)(2,1)} %collective-permute-done.14, bf16[64,640]{1,0:T(8,128)(2,1)} %collective-permute-done.13, bf16[64,640]{1,0:T(8,128)(2,1)S(1)} %collective-permute-done.12, bf16[4,64,640]{2,1,0:T(8,128)(2,1)S(1)} %fusion.11, ...), kind=kLoop, calls=%fused_computation.83 | loop fusion | flops 450560 | bytes 819204 | tf_op jit(solution)/shard_map/broadcast_in_dim | solution.py:274
  83.3 1.8 %fusion.45 = (f32[1,640,64]{1,2,0:T(8,128)}, f32[64,640]{1,0:T(8,128)S(1)}) fusion(f32[64,640]{1,0:T(8,128)S(1)} %get-tuple-element.112, f32[1,640,64]{1,2,0:T(8,128)} %param.19, f32[1,640,64]{1,2,0:T(8,128)S(1)} %copy-done.5, f32[1,640,64]{1,2,0:T(8,128)} %param.17), kind=kLoop, calls=%fused_computation.82 | loop fusion | flops 614400 | bytes 983040 | tf_op jit(solution)/shard_map/broadcast_in_dim | solution.py:272
  85.5 1.3 collective-permute-done.15
  88.2 1.8 %collective-permute-start.17 = (f32[32,512]{1,0:T(8,128)S(1)}, f32[32,512]{1,0:T(8,128)S(1)}, u32[]{:S(2)}, u32[]{:S(2)}) collective-permute-start(f32[32,512]{1,0:T(8,128)S(1)} %get-tuple-element.106), channel_id=1, source_target_pairs={{0,6},{1,7},{2,0},{3,1},{4,2},{5,3},{6,4},{7,5},{8,14},{9,15},{10,... | collective-permute-start | bytes 196616 | tf_op jit(solution)/shard_map/ppermute | solution.py:41
  90.0 1.8 %collective-permute-start.18 = (f32[32,512]{1,0:T(8,128)S(1)}, f32[32,512]{1,0:T(8,128)S(1)}, u32[]{:S(2)}, u32[]{:S(2)}) collective-permute-start(f32[32,512]{1,0:T(8,128)S(1)} %get-tuple-element.106), channel_id=1, source_target_pairs={{0,4},{1,5},{2,6},{3,7},{4,0},{5,1},{6,2},{7,3},{8,12},{9,13},{10,... | collective-permute-start | bytes 196616 | tf_op jit(solution)/shard_map/ppermute | solution.py:41
  92.6 3.2 %collective-permute-done.18 = f32[32,512]{1,0:T(8,128)S(1)} collective-permute-done((f32[32,512]{1,0:T(8,128)S(1)}, f32[32,512]{1,0:T(8,128)S(1)}, u32[]{:S(2)}, u32[]{:S(2)}) %collective-permute-start.18) | collective-permute-done | bytes 65568 | tf_op jit(solution)/shard_map/ppermute | solution.py:41
  95.9 2.9 %all-to-all-done.1 = bf16[8,64,1024]{2,1,0:T(8,128)(2,1)S(1)} async-done(((bf16[8,64,1024]{2,1,0:T(8,128)(2,1)}), bf16[8,64,1024]{2,1,0:T(8,128)(2,1)S(1)}, u32[]{:S(2)}, u32[]{:S(2)}) %all-to-all-start.1) | async-done | bytes 1048608 | tf_op jit(solution)/shard_map/all_to_all | solution.py:88
  100.0 1.5 %convolution_convert_fusion = bf16[512,1024]{1,0:T(8,128)(2,1)} fusion(f32[1,64,1024]{2,1,0:T(8,128)S(1)} %copy-done.7, f32[1,64,1024]{2,1,0:T(8,128)S(1)} %get-tuple-element.116, f32[1,64,1024]{2,1,0:T(8,128)S(1)} %copy-done.9, f32[1,64,1024]{2,1,0:T(8,128)S(1)} %copy-done.8, bf16[32,512]{1,0:T(8,128)(2,1)S(1)} %collective-permute-done.19, ...), kind=kOutput, calls=%fused_computation.7 | convolution fusion | flops 68976640 | bytes 2162689 | tf_op jit(solution)/shard_map/dot_general | solution.py:263
  101.5 8.1 %all-to-all-start.2 = ((bf16[32,16,1024]{2,1,0:T(8,128)(2,1)}), bf16[32,16,1024]{2,1,0:T(8,128)(2,1)S(1)}, u32[]{:S(2)}, u32[]{:S(2)}) async-start(bf16[32,16,1024]{2,1,0:T(8,128)(2,1)} %bitcast.49), calls=%async_computation.2 | async-start | bytes 2097152 | tf_op jit(solution)/shard_map/all_to_all | solution.py:266
  110.1 27.7 %all-to-all-done.2 = bf16[32,16,1024]{2,1,0:T(8,128)(2,1)S(1)} async-done(((bf16[32,16,1024]{2,1,0:T(8,128)(2,1)}), bf16[32,16,1024]{2,1,0:T(8,128)(2,1)S(1)}, u32[]{:S(2)}, u32[]{:S(2)}) %all-to-all-start.2) | async-done | bytes 1048608 | tf_op jit(solution)/shard_map/all_to_all | solution.py:266
  137.8 1.9 %copy-done.1 = bf16[2,128,1,48,128]{4,3,2,1,0:T(8,128)(2,1)S(1)} copy-done((bf16[2,128,1,48,128]{4,3,2,1,0:T(8,128)(2,1)S(1)}, bf16[2,128,1,48,128]{4,3,2,1,0:T(8,128)(2,1)}, u32[]{:S(2)}) %copy-start.1) | copy-done | bytes 3145752
  139.7 2.9 %shard_map.198 = bf16[128,1024]{1,0:T(8,128)(2,1)} custom-call(s32[128,1]{1,0:T(8,128)S(1)} %sub.31.place_ref, s32[128,1]{1,0:T(8,128)S(1)} %copy.42.length_ref, bf16[512,1024]{1,0:T(8,128)(2,1)S(1)} %bitcast.149, bf16[128,1024]{1,0:T(8,128)(2,1)S(1)} %copy-done.2, bf16[2,128,1,48,128]{4,3,2,1,0:T(8,128)(2,1)S(1)} %copy-done.1, ...), custom_call_target="tpu_custom_call" | custom-call | tf_op jit(solution)/shard_map/pallas_call | solution.py:184
  (68 shorter events, 12.4 us)
Async XLA Ops:
  0.6 12.0 %copy-start = (bf16[128,640]{1,0:T(8,128)(2,1)S(1)}, bf16[128,640]{1,0:T(8,128)(2,1)}, u32[]{:S(2)}) copy-start(bf16[128,640]{1,0:T(8,128)(2,1)} %param.26) | copy-start | bytes 491524
  0.6 13.2 %copy-start.4 = (bf16[1,32,640,64]{2,3,1,0:T(8,128)(2,1)S(1)}, bf16[1,32,640,64]{2,3,1,0:T(8,128)(2,1)}, u32[]{:S(2)}) copy-start(bf16[1,32,640,64]{2,3,1,0:T(8,128)(2,1)} %param.15) | copy-start | bytes 7864324
  1.9 12.0 %collective-permute-start = (bf16[2,64,640]{2,1,0:T(8,128)(2,1)S(1)}, bf16[2,64,640]{2,1,0:T(8,128)(2,1)S(1)}, u32[]{:S(2)}, u32[]{:S(2)}) collective-permute-start(bf16[2,64,640]{2,1,0:T(8,128)(2,1)S(1)} %get-tuple-element.59), channel_id=1, source_target_pairs={{0,32},{32,64},{64,96},{96,128},{128,160},{160,192},{192,224},{224... | collective-permute-start | bytes 491528 | tf_op jit(solution)/shard_map/ppermute | solution.py:36
  3.9 10.0 %collective-permute-start.1 = (bf16[2,64,640]{2,1,0:T(8,128)(2,1)S(1)}, bf16[2,64,640]{2,1,0:T(8,128)(2,1)S(1)}, u32[]{:S(2)}, u32[]{:S(2)}) collective-permute-start(bf16[2,64,640]{2,1,0:T(8,128)(2,1)S(1)} %get-tuple-element.60), channel_id=1, source_target_pairs={{0,224},{32,0},{64,32},{96,64},{128,96},{160,128},{192,160},{224,1... | collective-permute-start | bytes 491528 | tf_op jit(solution)/shard_map/ppermute | solution.py:36
  10.2 17.0 %collective-permute-start.4 = (bf16[4,64,1024]{2,1,0:T(8,128)(2,1)}, bf16[4,64,1024]{2,1,0:T(8,128)(2,1)}, u32[]{:S(2)}, u32[]{:S(2)}) collective-permute-start(bf16[4,64,1024]{2,1,0:T(8,128)(2,1)} %get-tuple-element.72), channel_id=1, source_target_pairs={{0,8},{8,16},{16,24},{24,0},{1,9},{9,17},{17,25},{25,1},{2,10},{10... | collective-permute-start | bytes 1572872 | tf_op jit(solution)/shard_map/ppermute | solution.py:36
  11.7 15.4 %collective-permute-start.5 = (bf16[4,64,1024]{2,1,0:T(8,128)(2,1)}, bf16[4,64,1024]{2,1,0:T(8,128)(2,1)}, u32[]{:S(2)}, u32[]{:S(2)}) collective-permute-start(bf16[4,64,1024]{2,1,0:T(8,128)(2,1)} %get-tuple-element.73), channel_id=1, source_target_pairs={{0,24},{8,0},{16,8},{24,16},{1,25},{9,1},{17,9},{25,17},{2,26},{10... | collective-permute-start | bytes 1572872 | tf_op jit(solution)/shard_map/ppermute | solution.py:36
  14.8 43.9 %all-to-all-start = ((bf16[32,16,640]{2,1,0:T(8,128)(2,1)}), bf16[32,16,640]{2,1,0:T(8,128)(2,1)S(1)}, u32[]{:S(2)}, u32[]{:S(2)}) async-start(bf16[32,16,640]{2,1,0:T(8,128)(2,1)} %bitcast.160), calls=%async_computation | async-start | bytes 1310720 | tf_op jit(solution)/shard_map/all_to_all | solution.py:241
  23.8 23.0 %collective-permute-start.2 = (bf16[4,64,640]{2,1,0:T(8,128)(2,1)}, bf16[4,64,640]{2,1,0:T(8,128)(2,1)}, u32[]{:S(2)}, u32[]{:S(2)}) collective-permute-start(bf16[4,64,640]{2,1,0:T(8,128)(2,1)} %get-tuple-element.68), channel_id=1, source_target_pairs={{0,32},{32,64},{64,96},{96,128},{128,160},{160,192},{192,224},{224... | collective-permute-start | bytes 983048 | tf_op jit(solution)/shard_map/ppermute | solution.py:36
  25.4 21.5 %collective-permute-start.3 = (bf16[4,64,640]{2,1,0:T(8,128)(2,1)}, bf16[4,64,640]{2,1,0:T(8,128)(2,1)}, u32[]{:S(2)}, u32[]{:S(2)}) collective-permute-start(bf16[4,64,640]{2,1,0:T(8,128)(2,1)} %get-tuple-element.69), channel_id=1, source_target_pairs={{0,224},{32,0},{64,32},{96,64},{128,96},{160,128},{192,160},{224,1... | collective-permute-start | bytes 983048 | tf_op jit(solution)/shard_map/ppermute | solution.py:36
  30.9 33.1 %collective-permute-start.10 = (bf16[8,64,1024]{2,1,0:T(8,128)(2,1)}, bf16[8,64,1024]{2,1,0:T(8,128)(2,1)}, u32[]{:S(2)}, u32[]{:S(2)}) collective-permute-start(bf16[8,64,1024]{2,1,0:T(8,128)(2,1)} %get-tuple-element.91), channel_id=1, source_target_pairs={{0,8},{8,16},{16,24},{24,0},{1,9},{9,17},{17,25},{25,1},{2,10},{10... | collective-permute-start | bytes 3145736 | tf_op jit(solution)/shard_map/ppermute | solution.py:36
  32.3 31.7 %collective-permute-start.11 = (bf16[8,64,1024]{2,1,0:T(8,128)(2,1)}, bf16[8,64,1024]{2,1,0:T(8,128)(2,1)}, u32[]{:S(2)}, u32[]{:S(2)}) collective-permute-start(bf16[8,64,1024]{2,1,0:T(8,128)(2,1)} %get-tuple-element.92), channel_id=1, source_target_pairs={{0,24},{8,0},{16,8},{24,16},{1,25},{9,1},{17,9},{25,17},{2,26},{10... | collective-permute-start | bytes 3145736 | tf_op jit(solution)/shard_map/ppermute | solution.py:36
  48.9 9.7 %collective-permute-start.6 = (bf16[4,64,640]{2,1,0:T(8,128)(2,1)}, bf16[4,64,640]{2,1,0:T(8,128)(2,1)}, u32[]{:S(2)}, u32[]{:S(2)}) collective-permute-start(bf16[4,64,640]{2,1,0:T(8,128)(2,1)} %get-tuple-element.81), channel_id=1, source_target_pairs={{0,32},{32,64},{64,96},{96,128},{128,160},{160,192},{192,224},{224... | collective-permute-start | bytes 983048 | tf_op jit(solution)/shard_map/ppermute | solution.py:36
  49.1 9.6 %collective-permute-start.7 = (bf16[4,64,640]{2,1,0:T(8,128)(2,1)}, bf16[4,64,640]{2,1,0:T(8,128)(2,1)}, u32[]{:S(2)}, u32[]{:S(2)}) collective-permute-start(bf16[4,64,640]{2,1,0:T(8,128)(2,1)} %get-tuple-element.82), channel_id=1, source_target_pairs={{0,224},{32,0},{64,32},{96,64},{128,96},{160,128},{192,160},{224,1... | collective-permute-start | bytes 983048 | tf_op jit(solution)/shard_map/ppermute | solution.py:36
  60.7 11.7 %collective-permute-start.8 = (bf16[4,64,640]{2,1,0:T(8,128)(2,1)}, bf16[4,64,640]{2,1,0:T(8,128)(2,1)S(1)}, u32[]{:S(2)}, u32[]{:S(2)}) collective-permute-start(bf16[4,64,640]{2,1,0:T(8,128)(2,1)} %get-tuple-element.87), channel_id=1, source_target_pairs={{0,32},{32,64},{64,96},{96,128},{128,160},{160,192},{192,224},{224... | collective-permute-start | bytes 983048 | tf_op jit(solution)/shard_map/ppermute | solution.py:36
  62.0 10.4 %collective-permute-start.9 = (bf16[4,64,640]{2,1,0:T(8,128)(2,1)}, bf16[4,64,640]{2,1,0:T(8,128)(2,1)S(1)}, u32[]{:S(2)}, u32[]{:S(2)}) collective-permute-start(bf16[4,64,640]{2,1,0:T(8,128)(2,1)} %get-tuple-element.88), channel_id=1, source_target_pairs={{0,224},{32,0},{64,32},{96,64},{128,96},{160,128},{192,160},{224,1... | collective-permute-start | bytes 983048 | tf_op jit(solution)/shard_map/ppermute | solution.py:36
  67.5 14.2 %copy-start.5 = (f32[1,640,64]{1,2,0:T(8,128)S(1)}, f32[1,640,64]{1,2,0:T(8,128)}, u32[]{:S(2)}) copy-start(f32[1,640,64]{1,2,0:T(8,128)} %param.21) | copy-start | bytes 491524
  67.5 31.3 %all-to-all-start.1 = ((bf16[8,64,1024]{2,1,0:T(8,128)(2,1)}), bf16[8,64,1024]{2,1,0:T(8,128)(2,1)S(1)}, u32[]{:S(2)}, u32[]{:S(2)}) async-start(bf16[8,64,1024]{2,1,0:T(8,128)(2,1)} %fusion.1), calls=%async_computation.1 | async-start | bytes 2097152 | tf_op jit(solution)/shard_map/all_to_all | solution.py:88
  73.6 25.3 %copy-start.7 = (f32[1,64,1024]{2,1,0:T(8,128)S(1)}, f32[1,64,1024]{2,1,0:T(8,128)}, u32[]{:S(2)}) copy-start(f32[1,64,1024]{2,1,0:T(8,128)} %param.18) | copy-start | bytes 786436
  73.6 25.3 %copy-start.8 = (f32[1,64,1024]{2,1,0:T(8,128)S(1)}, f32[1,64,1024]{2,1,0:T(8,128)}, u32[]{:S(2)}) copy-start(f32[1,64,1024]{2,1,0:T(8,128)} %param.20) | copy-start | bytes 786436
  73.6 25.3 %copy-start.9 = (f32[1,64,1024]{2,1,0:T(8,128)S(1)}, f32[1,64,1024]{2,1,0:T(8,128)}, u32[]{:S(2)}) copy-start(f32[1,64,1024]{2,1,0:T(8,128)} %param.22) | copy-start | bytes 786436
  73.6 4.7 %collective-permute-start.12 = (bf16[64,640]{1,0:T(8,128)(2,1)S(1)}, bf16[64,640]{1,0:T(8,128)(2,1)S(1)}, u32[]{:S(2)}, u32[]{:S(2)}) collective-permute-start(bf16[64,640]{1,0:T(8,128)(2,1)S(1)} %get-tuple-element.99), channel_id=1, source_target_pairs={{0,8},{8,16},{16,24},{24,0},{1,9},{9,17},{17,25},{25,1},{2,10},{10... | collective-permute-start | bytes 245768 | tf_op jit(solution)/shard_map/ppermute | solution.py:36
  75.5 6.2 %collective-permute-start.13 = (bf16[64,640]{1,0:T(8,128)(2,1)S(1)}, bf16[64,640]{1,0:T(8,128)(2,1)}, u32[]{:S(2)}, u32[]{:S(2)}) collective-permute-start(bf16[64,640]{1,0:T(8,128)(2,1)S(1)} %get-tuple-element.100), channel_id=1, source_target_pairs={{0,16},{8,24},{16,0},{24,8},{1,17},{9,25},{17,1},{25,9},{2,18},{10... | collective-permute-start | bytes 245768 | tf_op jit(solution)/shard_map/ppermute | solution.py:36
  76.3 5.4 %collective-permute-start.14 = (bf16[64,640]{1,0:T(8,128)(2,1)S(1)}, bf16[64,640]{1,0:T(8,128)(2,1)}, u32[]{:S(2)}, u32[]{:S(2)}) collective-permute-start(bf16[64,640]{1,0:T(8,128)(2,1)S(1)} %get-tuple-element.101), channel_id=1, source_target_pairs={{0,24},{8,0},{16,8},{24,16},{1,25},{9,1},{17,9},{25,17},{2,26},{10... | collective-permute-start | bytes 245768 | tf_op jit(solution)/shard_map/ppermute | solution.py:36
  85.1 14.9 %copy-start.6 = (f32[64,640]{1,0:T(8,128)}, f32[64,640]{1,0:T(8,128)S(1)}, u32[]{:S(2)}) copy-start(f32[64,640]{1,0:T(8,128)S(1)} %get-tuple-element.130) | copy-start | bytes 491524
  85.4 1.4 %collective-permute-start.15 = (f32[64,512]{1,0:T(8,128)S(1)}, f32[64,512]{1,0:T(8,128)S(1)}, u32[]{:S(2)}, u32[]{:S(2)}) collective-permute-start(f32[64,512]{1,0:T(8,128)S(1)} %fusion.37), channel_id=1, source_target_pairs={{0,1},{1,0},{2,3},{3,2},{4,5},{5,4},{6,7},{7,6},{8,9},{9,8},{10,11... | collective-permute-start | bytes 393224 | tf_op jit(solution)/shard_map/ppermute | solution.py:36
  86.9 5.4 %collective-permute-start.16 = (f32[32,512]{1,0:T(8,128)S(1)}, f32[32,512]{1,0:T(8,128)S(1)}, u32[]{:S(2)}, u32[]{:S(2)}) collective-permute-start(f32[32,512]{1,0:T(8,128)S(1)} %get-tuple-element.107), channel_id=1, source_target_pairs={{0,3},{1,2},{2,5},{3,4},{4,7},{5,6},{6,1},{7,0},{8,11},{9,10},{10,... | collective-permute-start | bytes 196616 | tf_op jit(solution)/shard_map/ppermute | solution.py:41
  88.2 4.4 %collective-permute-start.17 = (f32[32,512]{1,0:T(8,128)S(1)}, f32[32,512]{1,0:T(8,128)S(1)}, u32[]{:S(2)}, u32[]{:S(2)}) collective-permute-start(f32[32,512]{1,0:T(8,128)S(1)} %get-tuple-element.106), channel_id=1, source_target_pairs={{0,6},{1,7},{2,0},{3,1},{4,2},{5,3},{6,4},{7,5},{8,14},{9,15},{10,... | collective-permute-start | bytes 196616 | tf_op jit(solution)/shard_map/ppermute | solution.py:41
  90.0 5.8 %collective-permute-start.18 = (f32[32,512]{1,0:T(8,128)S(1)}, f32[32,512]{1,0:T(8,128)S(1)}, u32[]{:S(2)}, u32[]{:S(2)}) collective-permute-start(f32[32,512]{1,0:T(8,128)S(1)} %get-tuple-element.106), channel_id=1, source_target_pairs={{0,4},{1,5},{2,6},{3,7},{4,0},{5,1},{6,2},{7,3},{8,12},{9,13},{10,... | collective-permute-start | bytes 196616 | tf_op jit(solution)/shard_map/ppermute | solution.py:41
  95.8 4.2 %collective-permute-start.19 = (bf16[32,512]{1,0:T(8,128)(2,1)S(1)}, bf16[32,512]{1,0:T(8,128)(2,1)S(1)}, u32[]{:S(2)}, u32[]{:S(2)}) collective-permute-start(bf16[32,512]{1,0:T(8,128)(2,1)S(1)} %add_convert_fusion), channel_id=1, source_target_pairs={{0,1},{1,0},{2,3},{3,2},{4,5},{5,4},{6,7},{7,6},{8,9},{9,8},{10,11... | collective-permute-start | bytes 98312 | tf_op jit(solution)/shard_map/ppermute | solution.py:36
  100.0 37.8 %copy-start.2 = (bf16[128,1024]{1,0:T(8,128)(2,1)S(1)}, bf16[128,1024]{1,0:T(8,128)(2,1)}, u32[]{:S(2)}) copy-start(bf16[128,1024]{1,0:T(8,128)(2,1)} %frozen_ref.1) | copy-start | bytes 786436
  100.0 37.8 %copy-start.3 = (bf16[2,128,1,128]{3,1,2,0:T(8,128)(2,1)S(1)}, bf16[2,128,1,128]{3,1,2,0:T(8,128)(2,1)}, u32[]{:S(2)}) copy-start(bf16[2,128,1,128]{3,1,2,0:T(8,128)(2,1)} %param.29) | copy-start | bytes 196612
  101.5 36.2 %all-to-all-start.2 = ((bf16[32,16,1024]{2,1,0:T(8,128)(2,1)}), bf16[32,16,1024]{2,1,0:T(8,128)(2,1)S(1)}, u32[]{:S(2)}, u32[]{:S(2)}) async-start(bf16[32,16,1024]{2,1,0:T(8,128)(2,1)} %bitcast.49), calls=%async_computation.2 | async-start | bytes 2097152 | tf_op jit(solution)/shard_map/all_to_all | solution.py:266
  (4 other events, 35.1 us)
where the time goes:
time: 144 us; the launch traced here: 143 us
  waiting for transfers between devices  59.8 us (42%)
  starting transfers between devices  51.7 us (36%)
  other arithmetic  18.3 us (13%)
  local copies, waits for them, and re-layouts  5.98 us (4%)
  matrix products  3.03 us (2%)
  Pallas kernels  2.95 us (2%)
    all_to_all x1, waiting for transfers between devices, shards(): delta = lax.all_to_all(delta.reshape(policies, CAP, -1), ('z', 'y'), 0, 0)  27.7 us
    ppermute x17, waiting for transfers between devices, shift(): lax.ppermute(value, axis, [(i, (i + by) % size) for i in range(size)])  25.2 us
    ppermute x17, starting transfers between devices, shift(): lax.ppermute(value, axis, [(i, (i + by) % size) for i in range(size)])  24.7 us
    all_to_all x1, starting transfers between devices, shards(): lax.all_to_all(packed.reshape(policies, CAP, width), ('z', 'y'), 0, 0)  8.99 us
    convert_element_type x4, other arithmetic, step(): down = (self.chunk(-self.left).astype(F32) + down).astype(BF16)  8.83 us
    all_to_all x1, starting transfers between devices, shards(): delta = lax.all_to_all(delta.reshape(policies, CAP, -1), ('z', 'y'), 0, 0)  8.14 us
    all_to_all x1, starting transfers between devices, swapped_sum(): parts = lax.all_to_all(parts, axis, 0, 0)  4.95 us
    ppermute x3, starting transfers between devices, crossed(): return lax.ppermute(value, ('x', 'c'), pairs)  4.9 us
  transfers between devices with their start and end apart: 23, of which 9 were waited for; matrix products, arithmetic and copies ran while one was open for 16% of the time, Pallas kernels for 0%

commit v1 on v0

--- a/solution.py
+++ b/solution.py
@@ -107,18 +107,21 @@
     return total, sent
 
 
-def tensor_sum(value):
+def tensor_sum(value, state):
     core = lax.axis_index("c")
     both = (value + shift(value, "c", 1)).reshape(2, value.shape[0] // 2, value.shape[1])
     mine = lax.dynamic_index_in_dim(both, core, 0, keepdims=False)
     other = lax.dynamic_index_in_dim(both, 1 - core, 0, keepdims=False)
     mine, other = tied(mine, other)
     one, two, three = tied(crossed(other, 1, 1), crossed(mine, NX - 1, 0), crossed(mine, 2, 0))
+    new = adamw(*after(state, mine))
+    one, two, three = after((one, two, three), *new)
     total = ((mine + one) + (two + three)).astype(BF16)
     other = shift(total, "c", 1)
-    return jnp.where(
+    total = jnp.where(
         core == 0, jnp.concatenate([total, other], axis=0), jnp.concatenate([other, total], axis=0)
     )
+    return total, *new
 
 
 def decode_kernel(place_ref, length_ref, delta_ref, frozen_ref, cache_hbm, new_ref, out_ref, query, cache_ref, arrived):
@@ -146,6 +149,7 @@
     column = lax.broadcasted_iota(jnp.int32, (8, 8 * span), 1)
     first = lax.broadcasted_iota(jnp.int32, (8, 8 * span), 0) * span
     starts = range(base, base + block, 8)
+    new = new_ref[:, base : base + block, :].astype(F32)
     stack = lambda value: jnp.concatenate([value] * heads, axis=0)
     rows, scores, valid = [], [], []
     for low in starts:
@@ -162,7 +166,7 @@
         valid = (column >= first) & (column < first + length)
         bias = stack(jnp.where(valid, 0.0, -1e30))
         score = scores[i] * inverse + bias
-        own = jnp.sum(rows[i] * stack(new_ref[0, low : low + 8, :].astype(F32)), axis=1, keepdims=True) * inverse
+        own = jnp.sum(rows[i] * stack(new[0, 8 * i : 8 * i + 8]), axis=1, keepdims=True) * inverse
         peak = jnp.maximum(jnp.max(score, axis=1, keepdims=True), own)
         weights = jnp.exp(score - peak)
         own_weight = jnp.exp(own - peak)
@@ -172,7 +176,7 @@
     mixed = []
     for i, low in enumerate(starts):
         values = cache_ref[1, low : low + 8, 0].reshape(8 * span, width)
-        new_value = stack(new_ref[1, low : low + 8, :].astype(F32))
+        new_value = stack(new[1, 8 * i : 8 * i + 8])
         mixed.append(jnp.dot(probs[i], values, preferred_element_type=F32) + own_probs[i] * new_value)
     for h in range(heads):
         part = jnp.concatenate([value[8 * h : 8 * h + 8] for value in mixed], axis=0)
@@ -181,6 +185,7 @@
 
 def decode(place, length, delta, frozen, kv_cache, new_kv):
     vmem = pl.BlockSpec(memory_space=pltpu.VMEM)
+    kv_cache = pltpu.with_memory_space_constraint(kv_cache, pltpu.HBM)
     return pl.pallas_call(
         decode_kernel,
         in_specs=[vmem] * 4 + [pl.BlockSpec(memory_space=pltpu.HBM), vmem],
@@ -251,18 +256,17 @@
     grad_a, _ = sent_sum(ring_a.total(*after(come_a, sum_b)), "y")
     feats = feats.reshape(policies * CAP, width)
 
-    new_a, new_moment_a, new_second_a = adamw(
-        flip(adapter_a[0]), flip(moment_a[0]), flip(second_a[0]), grad_a
-    )
-    partial = lax.dot_general(
-        new_a.astype(BF16), feats, (((1,), (1,)), ((), ())), preferred_element_type=F32
-    )
-    shrink = tensor_sum(partial)
-
-    new_b, new_moment_b, new_second_b = adamw(adapter_b[0], moment_b[0], second_b[0], grad_b)
+    state_a = [flip(value[0]) for value in (adapter_a, moment_a, second_a)] + [grad_a]
+    page_a = adamw(*state_a)[0].astype(BF16)
+    partial = lax.dot_general(page_a, feats, (((1,), (1,)), ((), ())), preferred_element_type=F32)
+    shrink, new_a, new_moment_a, new_second_a = tensor_sum(partial, state_a)
+
+    state_b = [value[0] for value in (adapter_b, moment_b, second_b)] + [grad_b]
+    page_b = adamw(*state_b)[0].astype(BF16)
     delta = lax.dot_general(
-        shrink, new_b.astype(BF16), (((0,), (0,)), ((), ())), preferred_element_type=F32
+        shrink, page_b, (((0,), (0,)), ((), ())), preferred_element_type=F32
     ).astype(BF16)
+    new_b, new_moment_b, new_second_b = adamw(*after(state_b, delta))
     delta = lax.all_to_all(delta.reshape(policies, CAP, -1), ("z", "y"), 0, 0)
     delta = delta.reshape(policies * CAP, -1)
     attended = decode(place, cache_length, delta, frozen_query_output, kv_cache, new_kv)

time: 144 us -> 141 us (0.979)
  local copies, waits for them, and re-layouts: 5.98 us -> 4.1 us
  starting transfers between devices: 51.7 us -> 49.9 us
  other arithmetic: 18.3 us -> 16.8 us
    broadcast_in_dim x2 -> x1, other arithmetic: 3.43 us -> 1.07 us  [shards(): new_second_b[None]]
    unnamed x26, local copies, waits for them, and re-layouts: 1.96 us -> 0.07 us
    all_to_all x1, waiting for transfers between devices: 2.93 us -> 4.63 us  [swapped_sum(): parts = lax.all_to_all(parts, axis, 0, 0)]
  transfers between devices with their start and end apart: 23 -> 23, of which waited for: 9 -> 7; matrix products, arithmetic and copies ran while one was open for 16% -> 16% of each run, Pallas kernels for 0% -> 0%
where the time goes in v1:
time: 141 us
  waiting for transfers between devices  60.9 us (43%)
  starting transfers between devices  49.9 us (35%)
  other arithmetic  16.8 us (12%)
  local copies, waits for them, and re-layouts  4.1 us (3%)
  matrix products  3.93 us (3%)
  Pallas kernels  3.82 us (3%)
    all_to_all x1, waiting for transfers between devices, shards(): delta = lax.all_to_all(delta.reshape(policies, CAP, -1), ('z', 'y'), 0, 0)  26.9 us
    ppermute x17, waiting for transfers between devices, shift(): lax.ppermute(value, axis, [(i, (i + by) % size) for i in range(size)])  25.1 us
    ppermute x17, starting transfers between devices, shift(): lax.ppermute(value, axis, [(i, (i + by) % size) for i in range(size)])  24.7 us
    all_to_all x1, starting transfers between devices, shards(): lax.all_to_all(packed.reshape(policies, CAP, width), ('z', 'y'), 0, 0)  8.99 us
    convert_element_type x4, other arithmetic, step(): down = (self.chunk(-self.left).astype(F32) + down).astype(BF16)  8.85 us
    all_to_all x1, starting transfers between devices, shards(): delta = lax.all_to_all(delta.reshape(policies, CAP, -1), ('z', 'y'), 0, 0)  7.53 us
    all_to_all x1, starting transfers between devices, swapped_sum(): parts = lax.all_to_all(parts, axis, 0, 0)  4.95 us
    all_to_all x1, waiting for transfers between devices, swapped_sum(): parts = lax.all_to_all(parts, axis, 0, 0)  4.63 us
  transfers between devices with their start and end apart: 23, of which 7 were waited for; matrix products, arithmetic and copies ran while one was open for 16% of the time, Pallas kernels for 0%

profile of v1, /device:TPU:8, one launch (start us, length us, event | category | flops | bytes accessed | tf_op | source)
XLA Modules:
  0.0 140.5 jit_solution(12083152263288451296)
XLA Ops:
  0.7 1.2 dynamic-slice_bitcast_fusion.2
  1.9 2.0 %collective-permute-start = (bf16[2,64,640]{2,1,0:T(8,128)(2,1)S(1)}, bf16[2,64,640]{2,1,0:T(8,128)(2,1)S(1)}, u32[]{:S(2)}, u32[]{:S(2)}) collective-permute-start(bf16[2,64,640]{2,1,0:T(8,128)(2,1)S(1)} %get-tuple-element.70), channel_id=1, source_target_pairs={{0,32},{32,64},{64,96},{96,128},{128,160},{160,192},{192,224},{224... | collective-permute-start | bytes 491528 | tf_op jit(solution)/shard_map/ppermute | solution.py:36
  3.9 4.0 %collective-permute-start.1 = (bf16[2,64,640]{2,1,0:T(8,128)(2,1)S(1)}, bf16[2,64,640]{2,1,0:T(8,128)(2,1)S(1)}, u32[]{:S(2)}, u32[]{:S(2)}) collective-permute-start(bf16[2,64,640]{2,1,0:T(8,128)(2,1)S(1)} %get-tuple-element.71), channel_id=1, source_target_pairs={{0,224},{32,0},{64,32},{96,64},{128,96},{160,128},{192,160},{224,1... | collective-permute-start | bytes 491528 | tf_op jit(solution)/shard_map/ppermute | solution.py:36
  7.9 2.3 %dynamic-slice_bitcast_fusion = (bf16[4,64,1024]{2,1,0:T(8,128)(2,1)}, bf16[4,64,1024]{2,1,0:T(8,128)(2,1)}) fusion(bf16[8,4,64,1024]{3,2,1,0:T(8,128)(2,1)} %bitcast.133, s32[]{:T(128)S(6)} %select_n.77, s32[]{:T(128)S(6)} %add.346), kind=kLoop, calls=%fused_computation.24 | loop fusion | bytes 2097160 | tf_op jit(solution)/shard_map/slice | solution.py:69
  10.2 1.6 %collective-permute-start.4 = (bf16[4,64,1024]{2,1,0:T(8,128)(2,1)}, bf16[4,64,1024]{2,1,0:T(8,128)(2,1)}, u32[]{:S(2)}, u32[]{:S(2)}) collective-permute-start(bf16[4,64,1024]{2,1,0:T(8,128)(2,1)} %get-tuple-element.83), channel_id=1, source_target_pairs={{0,8},{8,16},{16,24},{24,0},{1,9},{9,17},{17,25},{25,1},{2,10},{10... | collective-permute-start | bytes 1572872 | tf_op jit(solution)/shard_map/ppermute | solution.py:36
  14.8 9.0 %all-to-all-start = ((bf16[32,16,640]{2,1,0:T(8,128)(2,1)}), bf16[32,16,640]{2,1,0:T(8,128)(2,1)S(1)}, u32[]{:S(2)}, u32[]{:S(2)}) async-start(bf16[32,16,640]{2,1,0:T(8,128)(2,1)} %bitcast.24), calls=%async_computation | async-start | bytes 1310720 | tf_op jit(solution)/shard_map/all_to_all | solution.py:246
  23.8 1.5 %collective-permute-start.2 = (bf16[4,64,640]{2,1,0:T(8,128)(2,1)}, bf16[4,64,640]{2,1,0:T(8,128)(2,1)}, u32[]{:S(2)}, u32[]{:S(2)}) collective-permute-start(bf16[4,64,640]{2,1,0:T(8,128)(2,1)} %get-tuple-element.79), channel_id=1, source_target_pairs={{0,32},{32,64},{64,96},{96,128},{128,160},{160,192},{192,224},{224... | collective-permute-start | bytes 983048 | tf_op jit(solution)/shard_map/ppermute | solution.py:36
  25.4 1.8 %collective-permute-start.3 = (bf16[4,64,640]{2,1,0:T(8,128)(2,1)}, bf16[4,64,640]{2,1,0:T(8,128)(2,1)}, u32[]{:S(2)}, u32[]{:S(2)}) collective-permute-start(bf16[4,64,640]{2,1,0:T(8,128)(2,1)} %get-tuple-element.80), channel_id=1, source_target_pairs={{0,224},{32,0},{64,32},{96,64},{128,96},{160,128},{192,160},{224,1... | collective-permute-start | bytes 983048 | tf_op jit(solution)/shard_map/ppermute | solution.py:36
  27.2 3.7 %fusion.2 = (bf16[8,64,1024]{2,1,0:T(8,128)(2,1)}, bf16[8,64,1024]{2,1,0:T(8,128)(2,1)}) fusion(bf16[4,64,1024]{2,1,0:T(8,128)(2,1)} %collective-permute-done.5, bf16[8,4,64,1024]{3,2,1,0:T(8,128)(2,1)} %bitcast.134, s32[]{:T(128)S(6)} %select_n.82, bf16[4,64,1024]{2,1,0:T(8,128)(2,1)} %collective-permute-done.4, s32[]{:T(128)S(6)} %select_n.81), kind=kLoop, calls=%fused_computation.4 | loop fusion | flops 4194304 | bytes 5242888 | tf_op jit(solution)/shard_map/convert_element_type | solution.py:80
  30.9 1.5 %collective-permute-start.10 = (bf16[8,64,1024]{2,1,0:T(8,128)(2,1)}, bf16[8,64,1024]{2,1,0:T(8,128)(2,1)}, u32[]{:S(2)}, u32[]{:S(2)}) collective-permute-start(bf16[8,64,1024]{2,1,0:T(8,128)(2,1)} %get-tuple-element.102), channel_id=1, source_target_pairs={{0,8},{8,16},{16,24},{24,0},{1,9},{9,17},{17,25},{25,1},{2,10},{10... | collective-permute-start | bytes 3145736 | tf_op jit(solution)/shard_map/ppermute | solution.py:36
  32.9 13.9 %collective-permute-done.2 = bf16[4,64,640]{2,1,0:T(8,128)(2,1)} collective-permute-done((bf16[4,64,640]{2,1,0:T(8,128)(2,1)}, bf16[4,64,640]{2,1,0:T(8,128)(2,1)}, u32[]{:S(2)}, u32[]{:S(2)}) %collective-permute-start.2) | collective-permute-done | bytes 327712 | tf_op jit(solution)/shard_map/ppermute | solution.py:36
  46.8 2.1 %fusion.5 = (bf16[4,64,640]{2,1,0:T(8,128)(2,1)}, bf16[4,64,640]{2,1,0:T(8,128)(2,1)}) fusion(bf16[4,64,640]{2,1,0:T(8,128)(2,1)} %collective-permute-done.3, bf16[8,4,64,640]{3,2,1,0:T(8,128)(2,1)S(1)} %bitcast.139, s32[]{:T(128)S(6)} %select_n.83, bf16[4,64,640]{2,1,0:T(8,128)(2,1)} %collective-permute-done.2, s32[]{:T(128)S(6)} %select_n.74), kind=kLoop, calls=%fused_computation.12 | loop fusion | flops 1310720 | bytes 1966088 | tf_op jit(solution)/shard_map/convert_element_type | solution.py:80
  49.1 3.1 %collective-permute-start.7 = (bf16[4,64,640]{2,1,0:T(8,128)(2,1)}, bf16[4,64,640]{2,1,0:T(8,128)(2,1)}, u32[]{:S(2)}, u32[]{:S(2)}) collective-permute-start(bf16[4,64,640]{2,1,0:T(8,128)(2,1)} %get-tuple-element.93), channel_id=1, source_target_pairs={{0,224},{32,0},{64,32},{96,64},{128,96},{160,128},{192,160},{224,1... | collective-permute-start | bytes 983048 | tf_op jit(solution)/shard_map/ppermute | solution.py:36
  52.2 6.5 %collective-permute-done.6 = bf16[4,64,640]{2,1,0:T(8,128)(2,1)} collective-permute-done((bf16[4,64,640]{2,1,0:T(8,128)(2,1)}, bf16[4,64,640]{2,1,0:T(8,128)(2,1)}, u32[]{:S(2)}, u32[]{:S(2)}) %collective-permute-start.6) | collective-permute-done | bytes 327712 | tf_op jit(solution)/shard_map/ppermute | solution.py:36
  58.7 2.1 %fusion.4 = (bf16[4,64,640]{2,1,0:T(8,128)(2,1)}, bf16[4,64,640]{2,1,0:T(8,128)(2,1)}) fusion(bf16[4,64,640]{2,1,0:T(8,128)(2,1)} %collective-permute-done.7, bf16[8,4,64,640]{3,2,1,0:T(8,128)(2,1)S(1)} %bitcast.140, s32[]{:T(128)S(6)} %select_n.84, bf16[4,64,640]{2,1,0:T(8,128)(2,1)} %collective-permute-done.6, s32[]{:T(128)S(6)} %select_n.73), kind=kLoop, calls=%fused_computation.10 | loop fusion | flops 1310720 | bytes 1966088 | tf_op jit(solution)/shard_map/convert_element_type | solution.py:80
  60.8 1.3 collective-permute-start.8
  62.1 1.9 %collective-permute-start.9 = (bf16[4,64,640]{2,1,0:T(8,128)(2,1)}, bf16[4,64,640]{2,1,0:T(8,128)(2,1)S(1)}, u32[]{:S(2)}, u32[]{:S(2)}) collective-permute-start(bf16[4,64,640]{2,1,0:T(8,128)(2,1)} %get-tuple-element.99), channel_id=1, source_target_pairs={{0,224},{32,0},{64,32},{96,64},{128,96},{160,128},{192,160},{224,1... | collective-permute-start | bytes 983048 | tf_op jit(solution)/shard_map/ppermute | solution.py:36
  64.0 3.5 %fusion.1 = bf16[8,64,1024]{2,1,0:T(8,128)(2,1)} fusion(bf16[8,64,1024]{2,1,0:T(8,128)(2,1)} %collective-permute-done.11, bf16[8,64,1024]{2,1,0:T(8,128)(2,1)} %collective-permute-done.10, bf16[8,4,64,1024]{3,2,1,0:T(8,128)(2,1)} %bitcast.135, s32[]{:T(128)S(6)} %select_n.85), kind=kLoop, calls=%fused_computation.2 | loop fusion | flops 3145728 | bytes 4194308 | tf_op jit(solution)/shard_map/convert_element_type | solution.py:84
  67.5 4.9 %all-to-all-start.1 = ((bf16[8,64,1024]{2,1,0:T(8,128)(2,1)}), bf16[8,64,1024]{2,1,0:T(8,128)(2,1)S(1)}, u32[]{:S(2)}, u32[]{:S(2)}) async-start(bf16[8,64,1024]{2,1,0:T(8,128)(2,1)} %fusion.1), calls=%async_computation.1 | async-start | bytes 2097152 | tf_op jit(solution)/shard_map/all_to_all | solution.py:88
  73.6 1.8 %collective-permute-start.12 = (bf16[64,640]{1,0:T(8,128)(2,1)S(1)}, bf16[64,640]{1,0:T(8,128)(2,1)S(1)}, u32[]{:S(2)}, u32[]{:S(2)}) collective-permute-start(bf16[64,640]{1,0:T(8,128)(2,1)S(1)} %get-tuple-element.110), channel_id=1, source_target_pairs={{0,8},{8,16},{16,24},{24,0},{1,9},{9,17},{17,25},{25,1},{2,10},{10... | collective-permute-start | bytes 245768 | tf_op jit(solution)/shard_map/ppermute | solution.py:36
  76.2 2.0 %collective-permute-start.14 = (bf16[64,640]{1,0:T(8,128)(2,1)S(1)}, bf16[64,640]{1,0:T(8,128)(2,1)S(1)}, u32[]{:S(2)}, u32[]{:S(2)}) collective-permute-start(bf16[64,640]{1,0:T(8,128)(2,1)S(1)} %get-tuple-element.112), channel_id=1, source_target_pairs={{0,24},{8,0},{16,8},{24,16},{1,25},{9,1},{17,9},{25,17},{2,26},{10... | collective-permute-start | bytes 245768 | tf_op jit(solution)/shard_map/ppermute | solution.py:36
  78.3 3.2 %collective-permute-done.13 = bf16[64,640]{1,0:T(8,128)(2,1)S(1)} collective-permute-done((bf16[64,640]{1,0:T(8,128)(2,1)S(1)}, bf16[64,640]{1,0:T(8,128)(2,1)S(1)}, u32[]{:S(2)}, u32[]{:S(2)}) %collective-permute-start.13) | collective-permute-done | bytes 81952 | tf_op jit(solution)/shard_map/ppermute | solution.py:36
  81.6 1.2 fusion.38
  83.0 1.3 collective-permute-done.15
  84.4 2.8 %collective-permute-start.17 = (f32[32,512]{1,0:T(8,128)S(1)}, f32[32,512]{1,0:T(8,128)S(1)}, u32[]{:S(2)}, u32[]{:S(2)}) collective-permute-start(f32[32,512]{1,0:T(8,128)S(1)} %get-tuple-element.117), channel_id=1, source_target_pairs={{0,6},{1,7},{2,0},{3,1},{4,2},{5,3},{6,4},{7,5},{8,14},{9,15},{10,... | collective-permute-start | bytes 196616 | tf_op jit(solution)/shard_map/ppermute | solution.py:41
  88.1 1.8 %multiply_subtract_fusion = (f32[64,640]{1,0:T(8,128)}, f32[64,640]{1,0:T(8,128)}, f32[64,640]{1,0:T(8,128)}) fusion(f32[64,640]{1,0:T(8,128)S(1)} %bitcast.146, f32[64,640]{1,0:T(8,128)S(1)} %fusion.27, f32[64,640]{1,0:T(8,128)S(1)} %bitcast.147, f32[64,640]{1,0:T(8,128)} %bitcast.148), kind=kLoop, calls=%fused_computation.54 | loop fusion | flops 614400 | bytes 1146880 | tf_op jit(solution)/shard_map/sub | solution.py:31
  89.8 4.2 %collective-permute-done.16 = f32[32,512]{1,0:T(8,128)S(1)} collective-permute-done((f32[32,512]{1,0:T(8,128)S(1)}, f32[32,512]{1,0:T(8,128)S(1)}, u32[]{:S(2)}, u32[]{:S(2)}) %collective-permute-start.16) | collective-permute-done | bytes 65568 | tf_op jit(solution)/shard_map/ppermute | solution.py:41
  94.2 4.6 %all-to-all-done.1 = bf16[8,64,1024]{2,1,0:T(8,128)(2,1)S(1)} async-done(((bf16[8,64,1024]{2,1,0:T(8,128)(2,1)}), bf16[8,64,1024]{2,1,0:T(8,128)(2,1)S(1)}, u32[]{:S(2)}, u32[]{:S(2)}) %all-to-all-start.1) | async-done | bytes 1048608 | tf_op jit(solution)/shard_map/all_to_all | solution.py:88
  99.1 1.5 %convolution_convert_fusion = bf16[512,1024]{1,0:T(8,128)(2,1)} fusion(f32[64,1024]{1,0:T(8,128)S(1)} %add_bitcast_fusion, bf16[32,512]{1,0:T(8,128)(2,1)S(1)} %collective-permute-done.19, bf16[32,512]{1,0:T(8,128)(2,1)S(1)} %add_convert_fusion, pred[]{:T(512)S(6)} %eq.35, f32[1,64,1024]{2,1,0:T(8,128)S(1)} %copy-done.4, f32[1,64,1024]{2,1,0:T(8,128)S(1)} %copy-done.6, ...), kind=kOutput, calls=%fused_computation.7 | convolution fusion | flops 68976640 | bytes 2162689 | tf_op jit(solution)/shard_map/dot_general | solution.py:266
  100.6 7.5 %all-to-all-start.2 = ((bf16[32,16,1024]{2,1,0:T(8,128)(2,1)}), bf16[32,16,1024]{2,1,0:T(8,128)(2,1)S(1)}, u32[]{:S(2)}, u32[]{:S(2)}) async-start(bf16[32,16,1024]{2,1,0:T(8,128)(2,1)} %bitcast.54), calls=%async_computation.2 | async-start | bytes 2097152 | tf_op jit(solution)/shard_map/all_to_all | solution.py:270
  109.6 26.9 %all-to-all-done.2 = bf16[32,16,1024]{2,1,0:T(8,128)(2,1)S(1)} async-done(((bf16[32,16,1024]{2,1,0:T(8,128)(2,1)}), bf16[32,16,1024]{2,1,0:T(8,128)(2,1)S(1)}, u32[]{:S(2)}, u32[]{:S(2)}) %all-to-all-start.2) | async-done | bytes 1048608 | tf_op jit(solution)/shard_map/all_to_all | solution.py:270
  136.5 3.8 %shard_map.198 = bf16[128,1024]{1,0:T(8,128)(2,1)} custom-call(s32[128,1]{1,0:T(8,128)S(1)} %sub.37.place_ref, s32[128,1]{1,0:T(8,128)S(1)} %copy.42.length_ref, bf16[512,1024]{1,0:T(8,128)(2,1)S(1)} %bitcast.131, bf16[128,1024]{1,0:T(8,128)(2,1)S(1)} %copy-done.1, bf16[2,128,1,48,128]{4,3,2,1,0:T(8,128)(2,1)} %cache_hbm.1, bf16[2,128,128]{2,1,0:T(8,128)(2,1)S(1)} %bitcast.132), custom_call_target="tpu_custom_call" | custom-call | tf_op jit(solution)/shard_map/pallas_call | solution.py:189
  (69 shorter events, 8.6 us)
Async XLA Ops:
  0.6 12.0 %copy-start = (bf16[128,640]{1,0:T(8,128)(2,1)S(1)}, bf16[128,640]{1,0:T(8,128)(2,1)}, u32[]{:S(2)}) copy-start(bf16[128,640]{1,0:T(8,128)(2,1)} %param.26) | copy-start | bytes 491524
  0.6 13.2 %copy-start.3 = (bf16[1,32,640,64]{2,3,1,0:T(8,128)(2,1)S(1)}, bf16[1,32,640,64]{2,3,1,0:T(8,128)(2,1)}, u32[]{:S(2)}) copy-start(bf16[1,32,640,64]{2,3,1,0:T(8,128)(2,1)} %param.15) | copy-start | bytes 7864324
  1.9 12.0 %collective-permute-start = (bf16[2,64,640]{2,1,0:T(8,128)(2,1)S(1)}, bf16[2,64,640]{2,1,0:T(8,128)(2,1)S(1)}, u32[]{:S(2)}, u32[]{:S(2)}) collective-permute-start(bf16[2,64,640]{2,1,0:T(8,128)(2,1)S(1)} %get-tuple-element.70), channel_id=1, source_target_pairs={{0,32},{32,64},{64,96},{96,128},{128,160},{160,192},{192,224},{224... | collective-permute-start | bytes 491528 | tf_op jit(solution)/shard_map/ppermute | solution.py:36
  3.9 10.0 %collective-permute-start.1 = (bf16[2,64,640]{2,1,0:T(8,128)(2,1)S(1)}, bf16[2,64,640]{2,1,0:T(8,128)(2,1)S(1)}, u32[]{:S(2)}, u32[]{:S(2)}) collective-permute-start(bf16[2,64,640]{2,1,0:T(8,128)(2,1)S(1)} %get-tuple-element.71), channel_id=1, source_target_pairs={{0,224},{32,0},{64,32},{96,64},{128,96},{160,128},{192,160},{224,1... | collective-permute-start | bytes 491528 | tf_op jit(solution)/shard_map/ppermute | solution.py:36
  10.2 17.0 %collective-permute-start.4 = (bf16[4,64,1024]{2,1,0:T(8,128)(2,1)}, bf16[4,64,1024]{2,1,0:T(8,128)(2,1)}, u32[]{:S(2)}, u32[]{:S(2)}) collective-permute-start(bf16[4,64,1024]{2,1,0:T(8,128)(2,1)} %get-tuple-element.83), channel_id=1, source_target_pairs={{0,8},{8,16},{16,24},{24,0},{1,9},{9,17},{17,25},{25,1},{2,10},{10... | collective-permute-start | bytes 1572872 | tf_op jit(solution)/shard_map/ppermute | solution.py:36
  11.8 15.4 %collective-permute-start.5 = (bf16[4,64,1024]{2,1,0:T(8,128)(2,1)}, bf16[4,64,1024]{2,1,0:T(8,128)(2,1)}, u32[]{:S(2)}, u32[]{:S(2)}) collective-permute-start(bf16[4,64,1024]{2,1,0:T(8,128)(2,1)} %get-tuple-element.84), channel_id=1, source_target_pairs={{0,24},{8,0},{16,8},{24,16},{1,25},{9,1},{17,9},{25,17},{2,26},{10... | collective-permute-start | bytes 1572872 | tf_op jit(solution)/shard_map/ppermute | solution.py:36
  14.8 43.9 %all-to-all-start = ((bf16[32,16,640]{2,1,0:T(8,128)(2,1)}), bf16[32,16,640]{2,1,0:T(8,128)(2,1)S(1)}, u32[]{:S(2)}, u32[]{:S(2)}) async-start(bf16[32,16,640]{2,1,0:T(8,128)(2,1)} %bitcast.24), calls=%async_computation | async-start | bytes 1310720 | tf_op jit(solution)/shard_map/all_to_all | solution.py:246
  23.8 23.0 %collective-permute-start.2 = (bf16[4,64,640]{2,1,0:T(8,128)(2,1)}, bf16[4,64,640]{2,1,0:T(8,128)(2,1)}, u32[]{:S(2)}, u32[]{:S(2)}) collective-permute-start(bf16[4,64,640]{2,1,0:T(8,128)(2,1)} %get-tuple-element.79), channel_id=1, source_target_pairs={{0,32},{32,64},{64,96},{96,128},{128,160},{160,192},{192,224},{224... | collective-permute-start | bytes 983048 | tf_op jit(solution)/shard_map/ppermute | solution.py:36
  25.4 21.5 %collective-permute-start.3 = (bf16[4,64,640]{2,1,0:T(8,128)(2,1)}, bf16[4,64,640]{2,1,0:T(8,128)(2,1)}, u32[]{:S(2)}, u32[]{:S(2)}) collective-permute-start(bf16[4,64,640]{2,1,0:T(8,128)(2,1)} %get-tuple-element.80), channel_id=1, source_target_pairs={{0,224},{32,0},{64,32},{96,64},{128,96},{160,128},{192,160},{224,1... | collective-permute-start | bytes 983048 | tf_op jit(solution)/shard_map/ppermute | solution.py:36
  30.9 33.1 %collective-permute-start.10 = (bf16[8,64,1024]{2,1,0:T(8,128)(2,1)}, bf16[8,64,1024]{2,1,0:T(8,128)(2,1)}, u32[]{:S(2)}, u32[]{:S(2)}) collective-permute-start(bf16[8,64,1024]{2,1,0:T(8,128)(2,1)} %get-tuple-element.102), channel_id=1, source_target_pairs={{0,8},{8,16},{16,24},{24,0},{1,9},{9,17},{17,25},{25,1},{2,10},{10... | collective-permute-start | bytes 3145736 | tf_op jit(solution)/shard_map/ppermute | solution.py:36
  32.3 31.7 %collective-permute-start.11 = (bf16[8,64,1024]{2,1,0:T(8,128)(2,1)}, bf16[8,64,1024]{2,1,0:T(8,128)(2,1)}, u32[]{:S(2)}, u32[]{:S(2)}) collective-permute-start(bf16[8,64,1024]{2,1,0:T(8,128)(2,1)} %get-tuple-element.103), channel_id=1, source_target_pairs={{0,24},{8,0},{16,8},{24,16},{1,25},{9,1},{17,9},{25,17},{2,26},{10... | collective-permute-start | bytes 3145736 | tf_op jit(solution)/shard_map/ppermute | solution.py:36
  48.9 9.7 %collective-permute-start.6 = (bf16[4,64,640]{2,1,0:T(8,128)(2,1)}, bf16[4,64,640]{2,1,0:T(8,128)(2,1)}, u32[]{:S(2)}, u32[]{:S(2)}) collective-permute-start(bf16[4,64,640]{2,1,0:T(8,128)(2,1)} %get-tuple-element.92), channel_id=1, source_target_pairs={{0,32},{32,64},{64,96},{96,128},{128,160},{160,192},{192,224},{224... | collective-permute-start | bytes 983048 | tf_op jit(solution)/shard_map/ppermute | solution.py:36
  49.1 9.6 %collective-permute-start.7 = (bf16[4,64,640]{2,1,0:T(8,128)(2,1)}, bf16[4,64,640]{2,1,0:T(8,128)(2,1)}, u32[]{:S(2)}, u32[]{:S(2)}) collective-permute-start(bf16[4,64,640]{2,1,0:T(8,128)(2,1)} %get-tuple-element.93), channel_id=1, source_target_pairs={{0,224},{32,0},{64,32},{96,64},{128,96},{160,128},{192,160},{224,1... | collective-permute-start | bytes 983048 | tf_op jit(solution)/shard_map/ppermute | solution.py:36
  60.8 11.7 %collective-permute-start.8 = (bf16[4,64,640]{2,1,0:T(8,128)(2,1)}, bf16[4,64,640]{2,1,0:T(8,128)(2,1)S(1)}, u32[]{:S(2)}, u32[]{:S(2)}) collective-permute-start(bf16[4,64,640]{2,1,0:T(8,128)(2,1)} %get-tuple-element.98), channel_id=1, source_target_pairs={{0,32},{32,64},{64,96},{96,128},{128,160},{160,192},{192,224},{224... | collective-permute-start | bytes 983048 | tf_op jit(solution)/shard_map/ppermute | solution.py:36
  62.1 10.4 %collective-permute-start.9 = (bf16[4,64,640]{2,1,0:T(8,128)(2,1)}, bf16[4,64,640]{2,1,0:T(8,128)(2,1)S(1)}, u32[]{:S(2)}, u32[]{:S(2)}) collective-permute-start(bf16[4,64,640]{2,1,0:T(8,128)(2,1)} %get-tuple-element.99), channel_id=1, source_target_pairs={{0,224},{32,0},{64,32},{96,64},{128,96},{160,128},{192,160},{224,1... | collective-permute-start | bytes 983048 | tf_op jit(solution)/shard_map/ppermute | solution.py:36
  67.5 14.1 %copy-start.8 = (f32[1,640,64]{1,2,0:T(8,128)S(1)}, f32[1,640,64]{1,2,0:T(8,128)}, u32[]{:S(2)}) copy-start(f32[1,640,64]{1,2,0:T(8,128)} %param.17) | copy-start | bytes 491524
  67.5 14.1 %copy-start.9 = (f32[1,640,64]{1,2,0:T(8,128)S(1)}, f32[1,640,64]{1,2,0:T(8,128)}, u32[]{:S(2)}) copy-start(f32[1,640,64]{1,2,0:T(8,128)} %param.19) | copy-start | bytes 491524
  67.5 31.3 %all-to-all-start.1 = ((bf16[8,64,1024]{2,1,0:T(8,128)(2,1)}), bf16[8,64,1024]{2,1,0:T(8,128)(2,1)S(1)}, u32[]{:S(2)}, u32[]{:S(2)}) async-start(bf16[8,64,1024]{2,1,0:T(8,128)(2,1)} %fusion.1), calls=%async_computation.1 | async-start | bytes 2097152 | tf_op jit(solution)/shard_map/all_to_all | solution.py:88
  73.6 4.7 %collective-permute-start.12 = (bf16[64,640]{1,0:T(8,128)(2,1)S(1)}, bf16[64,640]{1,0:T(8,128)(2,1)S(1)}, u32[]{:S(2)}, u32[]{:S(2)}) collective-permute-start(bf16[64,640]{1,0:T(8,128)(2,1)S(1)} %get-tuple-element.110), channel_id=1, source_target_pairs={{0,8},{8,16},{16,24},{24,0},{1,9},{9,17},{17,25},{25,1},{2,10},{10... | collective-permute-start | bytes 245768 | tf_op jit(solution)/shard_map/ppermute | solution.py:36
  75.5 6.0 %collective-permute-start.13 = (bf16[64,640]{1,0:T(8,128)(2,1)S(1)}, bf16[64,640]{1,0:T(8,128)(2,1)S(1)}, u32[]{:S(2)}, u32[]{:S(2)}) collective-permute-start(bf16[64,640]{1,0:T(8,128)(2,1)S(1)} %get-tuple-element.111), channel_id=1, source_target_pairs={{0,16},{8,24},{16,0},{24,8},{1,17},{9,25},{17,1},{25,9},{2,18},{10... | collective-permute-start | bytes 245768 | tf_op jit(solution)/shard_map/ppermute | solution.py:36
  76.2 5.3 %collective-permute-start.14 = (bf16[64,640]{1,0:T(8,128)(2,1)S(1)}, bf16[64,640]{1,0:T(8,128)(2,1)S(1)}, u32[]{:S(2)}, u32[]{:S(2)}) collective-permute-start(bf16[64,640]{1,0:T(8,128)(2,1)S(1)} %get-tuple-element.112), channel_id=1, source_target_pairs={{0,24},{8,0},{16,8},{24,16},{1,25},{9,1},{17,9},{25,17},{2,26},{10... | collective-permute-start | bytes 245768 | tf_op jit(solution)/shard_map/ppermute | solution.py:36
  82.9 16.2 %copy-start.4 = (f32[1,64,1024]{2,1,0:T(8,128)S(1)}, f32[1,64,1024]{2,1,0:T(8,128)}, u32[]{:S(2)}) copy-start(f32[1,64,1024]{2,1,0:T(8,128)} %param.22) | copy-start | bytes 786436
  82.9 16.2 %copy-start.5 = (f32[1,64,1024]{2,1,0:T(8,128)S(1)}, f32[1,64,1024]{2,1,0:T(8,128)}, u32[]{:S(2)}) copy-start(f32[1,64,1024]{2,1,0:T(8,128)} %param.18) | copy-start | bytes 786436
  82.9 16.2 %copy-start.6 = (f32[1,64,1024]{2,1,0:T(8,128)S(1)}, f32[1,64,1024]{2,1,0:T(8,128)}, u32[]{:S(2)}) copy-start(f32[1,64,1024]{2,1,0:T(8,128)} %param.20) | copy-start | bytes 786436
  82.9 1.4 %collective-permute-start.15 = (f32[64,512]{1,0:T(8,128)S(1)}, f32[64,512]{1,0:T(8,128)S(1)}, u32[]{:S(2)}, u32[]{:S(2)}) collective-permute-start(f32[64,512]{1,0:T(8,128)S(1)} %fusion.38), channel_id=1, source_target_pairs={{0,1},{1,0},{2,3},{3,2},{4,5},{5,4},{6,7},{7,6},{8,9},{9,8},{10,11... | collective-permute-start | bytes 393224 | tf_op jit(solution)/shard_map/ppermute | solution.py:36
  84.4 9.7 %collective-permute-start.17 = (f32[32,512]{1,0:T(8,128)S(1)}, f32[32,512]{1,0:T(8,128)S(1)}, u32[]{:S(2)}, u32[]{:S(2)}) collective-permute-start(f32[32,512]{1,0:T(8,128)S(1)} %get-tuple-element.117), channel_id=1, source_target_pairs={{0,6},{1,7},{2,0},{3,1},{4,2},{5,3},{6,4},{7,5},{8,14},{9,15},{10,... | collective-permute-start | bytes 196616 | tf_op jit(solution)/shard_map/ppermute | solution.py:41
  87.2 6.9 %collective-permute-start.18 = (f32[32,512]{1,0:T(8,128)S(1)}, f32[32,512]{1,0:T(8,128)S(1)}, u32[]{:S(2)}, u32[]{:S(2)}) collective-permute-start(f32[32,512]{1,0:T(8,128)S(1)} %get-tuple-element.117), channel_id=1, source_target_pairs={{0,4},{1,5},{2,6},{3,7},{4,0},{5,1},{6,2},{7,3},{8,12},{9,13},{10,... | collective-permute-start | bytes 196616 | tf_op jit(solution)/shard_map/ppermute | solution.py:41
  88.0 6.1 %collective-permute-start.16 = (f32[32,512]{1,0:T(8,128)S(1)}, f32[32,512]{1,0:T(8,128)S(1)}, u32[]{:S(2)}, u32[]{:S(2)}) collective-permute-start(f32[32,512]{1,0:T(8,128)S(1)} %get-tuple-element.122), channel_id=1, source_target_pairs={{0,3},{1,2},{2,5},{3,4},{4,7},{5,6},{6,1},{7,0},{8,11},{9,10},{10,... | collective-permute-start | bytes 196616 | tf_op jit(solution)/shard_map/ppermute | solution.py:41
  94.1 4.9 %collective-permute-start.19 = (bf16[32,512]{1,0:T(8,128)(2,1)S(1)}, bf16[32,512]{1,0:T(8,128)(2,1)S(1)}, u32[]{:S(2)}, u32[]{:S(2)}) collective-permute-start(bf16[32,512]{1,0:T(8,128)(2,1)S(1)} %add_convert_fusion), channel_id=1, source_target_pairs={{0,1},{1,0},{2,3},{3,2},{4,5},{5,4},{6,7},{7,6},{8,9},{9,8},{10,11... | collective-permute-start | bytes 98312 | tf_op jit(solution)/shard_map/ppermute | solution.py:36
  100.6 35.9 %copy-start.1 = (bf16[128,1024]{1,0:T(8,128)(2,1)S(1)}, bf16[128,1024]{1,0:T(8,128)(2,1)}, u32[]{:S(2)}) copy-start(bf16[128,1024]{1,0:T(8,128)(2,1)} %frozen_ref.1) | copy-start | bytes 786436
  100.6 35.9 %copy-start.2 = (bf16[2,128,1,128]{3,1,2,0:T(8,128)(2,1)S(1)}, bf16[2,128,1,128]{3,1,2,0:T(8,128)(2,1)}, u32[]{:S(2)}) copy-start(bf16[2,128,1,128]{3,1,2,0:T(8,128)(2,1)} %param.29) | copy-start | bytes 196612
  100.6 35.9 %all-to-all-start.2 = ((bf16[32,16,1024]{2,1,0:T(8,128)(2,1)}), bf16[32,16,1024]{2,1,0:T(8,128)(2,1)S(1)}, u32[]{:S(2)}, u32[]{:S(2)}) async-start(bf16[32,16,1024]{2,1,0:T(8,128)(2,1)} %bitcast.54), calls=%async_computation.2 | async-start | bytes 2097152 | tf_op jit(solution)/shard_map/all_to_all | solution.py:270
  (4 other events, 42.1 us)

commit v2 on v1

--- a/solution.py
+++ b/solution.py
@@ -113,9 +113,10 @@
     mine = lax.dynamic_index_in_dim(both, core, 0, keepdims=False)
     other = lax.dynamic_index_in_dim(both, 1 - core, 0, keepdims=False)
     mine, other = tied(mine, other)
-    one, two, three = tied(crossed(other, 1, 1), crossed(mine, NX - 1, 0), crossed(mine, 2, 0))
+    sent, other = mine.astype(BF16), other.astype(BF16)
+    one, two, three = tied(crossed(other, 1, 1), crossed(sent, NX - 1, 0), crossed(sent, 2, 0))
     new = adamw(*after(state, mine))
-    one, two, three = after((one, two, three), *new)
+    one, two, three = [part.astype(F32) for part in after((one, two, three), *new)]
     total = ((mine + one) + (two + three)).astype(BF16)
     other = shift(total, "c", 1)
     total = jnp.where(

time: 141 us -> 141 us (level)
  waiting for transfers between devices: 60.9 us -> 59.3 us
where the time goes in v2:
time: 141 us; the launch traced here: 140 us
  waiting for transfers between devices  59.3 us (42%)
  starting transfers between devices  49.8 us (35%)
  other arithmetic  17.7 us (13%)
  local copies, waits for them, and re-layouts  4.67 us (3%)
  matrix products  4.02 us (3%)
  Pallas kernels  3.82 us (3%)
    all_to_all x1, waiting for transfers between devices, shards(): delta = lax.all_to_all(delta.reshape(policies, CAP, -1), ('z', 'y'), 0, 0)  26.9 us
    ppermute x17, starting transfers between devices, shift(): lax.ppermute(value, axis, [(i, (i + by) % size) for i in range(size)])  24.7 us
    ppermute x17, waiting for transfers between devices, shift(): lax.ppermute(value, axis, [(i, (i + by) % size) for i in range(size)])  24.5 us
    all_to_all x1, starting transfers between devices, shards(): lax.all_to_all(packed.reshape(policies, CAP, width), ('z', 'y'), 0, 0)  8.99 us
    convert_element_type x4, other arithmetic, step(): down = (self.chunk(-self.left).astype(F32) + down).astype(BF16)  8.83 us
    all_to_all x1, starting transfers between devices, shards(): delta = lax.all_to_all(delta.reshape(policies, CAP, -1), ('z', 'y'), 0, 0)  7.46 us
    all_to_all x1, starting transfers between devices, swapped_sum(): parts = lax.all_to_all(parts, axis, 0, 0)  4.95 us
    all_to_all x1, waiting for transfers between devices, swapped_sum(): parts = lax.all_to_all(parts, axis, 0, 0)  4.66 us
  transfers between devices with their start and end apart: 23, of which 7 were waited for; matrix products, arithmetic and copies ran while one was open for 16% of the time, Pallas kernels for 0%

profile of v2, /device:TPU:8, one launch (start us, length us, event | category | flops | bytes accessed | tf_op | source)
XLA Modules:
  0.0 140.5 jit_solution(1283397679419884214)
XLA Ops:
  0.7 1.2 dynamic-slice_bitcast_fusion.2
  1.9 2.0 %collective-permute-start = (bf16[2,64,640]{2,1,0:T(8,128)(2,1)S(1)}, bf16[2,64,640]{2,1,0:T(8,128)(2,1)S(1)}, u32[]{:S(2)}, u32[]{:S(2)}) collective-permute-start(bf16[2,64,640]{2,1,0:T(8,128)(2,1)S(1)} %get-tuple-element.70), channel_id=1, source_target_pairs={{0,32},{32,64},{64,96},{96,128},{128,160},{160,192},{192,224},{224... | collective-permute-start | bytes 491528 | tf_op jit(solution)/shard_map/ppermute | solution.py:36
  3.9 4.0 %collective-permute-start.1 = (bf16[2,64,640]{2,1,0:T(8,128)(2,1)S(1)}, bf16[2,64,640]{2,1,0:T(8,128)(2,1)S(1)}, u32[]{:S(2)}, u32[]{:S(2)}) collective-permute-start(bf16[2,64,640]{2,1,0:T(8,128)(2,1)S(1)} %get-tuple-element.71), channel_id=1, source_target_pairs={{0,224},{32,0},{64,32},{96,64},{128,96},{160,128},{192,160},{224,1... | collective-permute-start | bytes 491528 | tf_op jit(solution)/shard_map/ppermute | solution.py:36
  7.9 2.3 %dynamic-slice_bitcast_fusion = (bf16[4,64,1024]{2,1,0:T(8,128)(2,1)}, bf16[4,64,1024]{2,1,0:T(8,128)(2,1)}) fusion(bf16[8,4,64,1024]{3,2,1,0:T(8,128)(2,1)} %bitcast.133, s32[]{:T(128)S(6)} %select_n.77, s32[]{:T(128)S(6)} %add.346), kind=kLoop, calls=%fused_computation.24 | loop fusion | bytes 2097160 | tf_op jit(solution)/shard_map/slice | solution.py:69
  10.2 1.6 %collective-permute-start.4 = (bf16[4,64,1024]{2,1,0:T(8,128)(2,1)}, bf16[4,64,1024]{2,1,0:T(8,128)(2,1)}, u32[]{:S(2)}, u32[]{:S(2)}) collective-permute-start(bf16[4,64,1024]{2,1,0:T(8,128)(2,1)} %get-tuple-element.83), channel_id=1, source_target_pairs={{0,8},{8,16},{16,24},{24,0},{1,9},{9,17},{17,25},{25,1},{2,10},{10... | collective-permute-start | bytes 1572872 | tf_op jit(solution)/shard_map/ppermute | solution.py:36
  12.7 1.2 convolution_convert_fusion.1
  14.8 9.0 %all-to-all-start = ((bf16[32,16,640]{2,1,0:T(8,128)(2,1)}), bf16[32,16,640]{2,1,0:T(8,128)(2,1)S(1)}, u32[]{:S(2)}, u32[]{:S(2)}) async-start(bf16[32,16,640]{2,1,0:T(8,128)(2,1)} %bitcast.24), calls=%async_computation | async-start | bytes 1310720 | tf_op jit(solution)/shard_map/all_to_all | solution.py:247
  23.8 1.5 %collective-permute-start.2 = (bf16[4,64,640]{2,1,0:T(8,128)(2,1)}, bf16[4,64,640]{2,1,0:T(8,128)(2,1)}, u32[]{:S(2)}, u32[]{:S(2)}) collective-permute-start(bf16[4,64,640]{2,1,0:T(8,128)(2,1)} %get-tuple-element.79), channel_id=1, source_target_pairs={{0,32},{32,64},{64,96},{96,128},{128,160},{160,192},{192,224},{224... | collective-permute-start | bytes 983048 | tf_op jit(solution)/shard_map/ppermute | solution.py:36
  25.3 1.8 %collective-permute-start.3 = (bf16[4,64,640]{2,1,0:T(8,128)(2,1)}, bf16[4,64,640]{2,1,0:T(8,128)(2,1)}, u32[]{:S(2)}, u32[]{:S(2)}) collective-permute-start(bf16[4,64,640]{2,1,0:T(8,128)(2,1)} %get-tuple-element.80), channel_id=1, source_target_pairs={{0,224},{32,0},{64,32},{96,64},{128,96},{160,128},{192,160},{224,1... | collective-permute-start | bytes 983048 | tf_op jit(solution)/shard_map/ppermute | solution.py:36
  27.1 3.7 %fusion.2 = (bf16[8,64,1024]{2,1,0:T(8,128)(2,1)}, bf16[8,64,1024]{2,1,0:T(8,128)(2,1)}) fusion(bf16[4,64,1024]{2,1,0:T(8,128)(2,1)} %collective-permute-done.5, bf16[8,4,64,1024]{3,2,1,0:T(8,128)(2,1)} %bitcast.134, s32[]{:T(128)S(6)} %select_n.82, bf16[4,64,1024]{2,1,0:T(8,128)(2,1)} %collective-permute-done.4, s32[]{:T(128)S(6)} %select_n.81), kind=kLoop, calls=%fused_computation.4 | loop fusion | flops 4194304 | bytes 5242888 | tf_op jit(solution)/shard_map/convert_element_type | solution.py:80
  30.9 1.5 %collective-permute-start.10 = (bf16[8,64,1024]{2,1,0:T(8,128)(2,1)}, bf16[8,64,1024]{2,1,0:T(8,128)(2,1)}, u32[]{:S(2)}, u32[]{:S(2)}) collective-permute-start(bf16[8,64,1024]{2,1,0:T(8,128)(2,1)} %get-tuple-element.102), channel_id=1, source_target_pairs={{0,8},{8,16},{16,24},{24,0},{1,9},{9,17},{17,25},{25,1},{2,10},{10... | collective-permute-start | bytes 3145736 | tf_op jit(solution)/shard_map/ppermute | solution.py:36
  32.9 13.9 %collective-permute-done.2 = bf16[4,64,640]{2,1,0:T(8,128)(2,1)} collective-permute-done((bf16[4,64,640]{2,1,0:T(8,128)(2,1)}, bf16[4,64,640]{2,1,0:T(8,128)(2,1)}, u32[]{:S(2)}, u32[]{:S(2)}) %collective-permute-start.2) | collective-permute-done | bytes 327712 | tf_op jit(solution)/shard_map/ppermute | solution.py:36
  46.8 2.1 %fusion.5 = (bf16[4,64,640]{2,1,0:T(8,128)(2,1)}, bf16[4,64,640]{2,1,0:T(8,128)(2,1)}) fusion(bf16[4,64,640]{2,1,0:T(8,128)(2,1)} %collective-permute-done.3, bf16[8,4,64,640]{3,2,1,0:T(8,128)(2,1)S(1)} %bitcast.139, s32[]{:T(128)S(6)} %select_n.83, bf16[4,64,640]{2,1,0:T(8,128)(2,1)} %collective-permute-done.2, s32[]{:T(128)S(6)} %select_n.74), kind=kLoop, calls=%fused_computation.12 | loop fusion | flops 1310720 | bytes 1966088 | tf_op jit(solution)/shard_map/convert_element_type | solution.py:80
  49.1 3.1 %collective-permute-start.7 = (bf16[4,64,640]{2,1,0:T(8,128)(2,1)}, bf16[4,64,640]{2,1,0:T(8,128)(2,1)}, u32[]{:S(2)}, u32[]{:S(2)}) collective-permute-start(bf16[4,64,640]{2,1,0:T(8,128)(2,1)} %get-tuple-element.93), channel_id=1, source_target_pairs={{0,224},{32,0},{64,32},{96,64},{128,96},{160,128},{192,160},{224,1... | collective-permute-start | bytes 983048 | tf_op jit(solution)/shard_map/ppermute | solution.py:36
  52.1 6.5 %collective-permute-done.6 = bf16[4,64,640]{2,1,0:T(8,128)(2,1)} collective-permute-done((bf16[4,64,640]{2,1,0:T(8,128)(2,1)}, bf16[4,64,640]{2,1,0:T(8,128)(2,1)}, u32[]{:S(2)}, u32[]{:S(2)}) %collective-permute-start.6) | collective-permute-done | bytes 327712 | tf_op jit(solution)/shard_map/ppermute | solution.py:36
  58.6 2.1 %fusion.4 = (bf16[4,64,640]{2,1,0:T(8,128)(2,1)}, bf16[4,64,640]{2,1,0:T(8,128)(2,1)}) fusion(bf16[4,64,640]{2,1,0:T(8,128)(2,1)} %collective-permute-done.7, bf16[8,4,64,640]{3,2,1,0:T(8,128)(2,1)S(1)} %bitcast.140, s32[]{:T(128)S(6)} %select_n.84, bf16[4,64,640]{2,1,0:T(8,128)(2,1)} %collective-permute-done.6, s32[]{:T(128)S(6)} %select_n.73), kind=kLoop, calls=%fused_computation.10 | loop fusion | flops 1310720 | bytes 1966088 | tf_op jit(solution)/shard_map/convert_element_type | solution.py:80
  60.7 1.3 collective-permute-start.8
  62.0 1.9 %collective-permute-start.9 = (bf16[4,64,640]{2,1,0:T(8,128)(2,1)}, bf16[4,64,640]{2,1,0:T(8,128)(2,1)S(1)}, u32[]{:S(2)}, u32[]{:S(2)}) collective-permute-start(bf16[4,64,640]{2,1,0:T(8,128)(2,1)} %get-tuple-element.99), channel_id=1, source_target_pairs={{0,224},{32,0},{64,32},{96,64},{128,96},{160,128},{192,160},{224,1... | collective-permute-start | bytes 983048 | tf_op jit(solution)/shard_map/ppermute | solution.py:36
  64.0 3.5 %fusion.1 = bf16[8,64,1024]{2,1,0:T(8,128)(2,1)} fusion(bf16[8,64,1024]{2,1,0:T(8,128)(2,1)} %collective-permute-done.11, bf16[8,64,1024]{2,1,0:T(8,128)(2,1)} %collective-permute-done.10, bf16[8,4,64,1024]{3,2,1,0:T(8,128)(2,1)} %bitcast.135, s32[]{:T(128)S(6)} %select_n.85), kind=kLoop, calls=%fused_computation.2 | loop fusion | flops 3145728 | bytes 4194308 | tf_op jit(solution)/shard_map/convert_element_type | solution.py:84
  67.5 4.9 %all-to-all-start.1 = ((bf16[8,64,1024]{2,1,0:T(8,128)(2,1)}), bf16[8,64,1024]{2,1,0:T(8,128)(2,1)S(1)}, u32[]{:S(2)}, u32[]{:S(2)}) async-start(bf16[8,64,1024]{2,1,0:T(8,128)(2,1)} %fusion.1), calls=%async_computation.1 | async-start | bytes 2097152 | tf_op jit(solution)/shard_map/all_to_all | solution.py:88
  73.6 1.8 %collective-permute-start.12 = (bf16[64,640]{1,0:T(8,128)(2,1)S(1)}, bf16[64,640]{1,0:T(8,128)(2,1)S(1)}, u32[]{:S(2)}, u32[]{:S(2)}) collective-permute-start(bf16[64,640]{1,0:T(8,128)(2,1)S(1)} %get-tuple-element.110), channel_id=1, source_target_pairs={{0,8},{8,16},{16,24},{24,0},{1,9},{9,17},{17,25},{25,1},{2,10},{10... | collective-permute-start | bytes 245768 | tf_op jit(solution)/shard_map/ppermute | solution.py:36
  76.2 2.0 %collective-permute-start.14 = (bf16[64,640]{1,0:T(8,128)(2,1)S(1)}, bf16[64,640]{1,0:T(8,128)(2,1)S(1)}, u32[]{:S(2)}, u32[]{:S(2)}) collective-permute-start(bf16[64,640]{1,0:T(8,128)(2,1)S(1)} %get-tuple-element.112), channel_id=1, source_target_pairs={{0,24},{8,0},{16,8},{24,16},{1,25},{9,1},{17,9},{25,17},{2,26},{10... | collective-permute-start | bytes 245768 | tf_op jit(solution)/shard_map/ppermute | solution.py:36
  78.2 3.2 %collective-permute-done.13 = bf16[64,640]{1,0:T(8,128)(2,1)S(1)} collective-permute-done((bf16[64,640]{1,0:T(8,128)(2,1)S(1)}, bf16[64,640]{1,0:T(8,128)(2,1)S(1)}, u32[]{:S(2)}, u32[]{:S(2)}) %collective-permute-start.13) | collective-permute-done | bytes 81952 | tf_op jit(solution)/shard_map/ppermute | solution.py:36
  81.6 1.3 fusion.38
  85.4 2.8 %collective-permute-start.17 = (bf16[32,512]{1,0:T(8,128)(2,1)S(1)}, bf16[32,512]{1,0:T(8,128)(2,1)S(1)}, u32[]{:S(2)}, u32[]{:S(2)}) collective-permute-start(bf16[32,512]{1,0:T(8,128)(2,1)S(1)} %convert_element_type.254), channel_id=1, source_target_pairs={{0,6},{1,7},{2,0},{3,1},{4,2},{5,3},{6,4},{7,5},{8,14},{9,15},{10,... | collective-permute-start | bytes 98312 | tf_op jit(solution)/shard_map/ppermute | solution.py:41
  89.1 1.8 %multiply_subtract_fusion = (f32[64,640]{1,0:T(8,128)}, f32[64,640]{1,0:T(8,128)}, f32[64,640]{1,0:T(8,128)}) fusion(f32[64,640]{1,0:T(8,128)S(1)} %bitcast.147, f32[64,640]{1,0:T(8,128)S(1)} %fusion.27, f32[64,640]{1,0:T(8,128)S(1)} %bitcast.148, f32[64,640]{1,0:T(8,128)} %bitcast.149), kind=kLoop, calls=%fused_computation.54 | loop fusion | flops 614400 | bytes 1146880 | tf_op jit(solution)/shard_map/sub | solution.py:31
  90.8 3.2 %collective-permute-done.16 = bf16[32,512]{1,0:T(8,128)(2,1)S(1)} collective-permute-done((bf16[32,512]{1,0:T(8,128)(2,1)S(1)}, bf16[32,512]{1,0:T(8,128)(2,1)S(1)}, u32[]{:S(2)}, u32[]{:S(2)}) %collective-permute-start.16) | collective-permute-done | bytes 32800 | tf_op jit(solution)/shard_map/ppermute | solution.py:41
  94.2 4.7 %all-to-all-done.1 = bf16[8,64,1024]{2,1,0:T(8,128)(2,1)S(1)} async-done(((bf16[8,64,1024]{2,1,0:T(8,128)(2,1)}), bf16[8,64,1024]{2,1,0:T(8,128)(2,1)S(1)}, u32[]{:S(2)}, u32[]{:S(2)}) %all-to-all-start.1) | async-done | bytes 1048608 | tf_op jit(solution)/shard_map/all_to_all | solution.py:88
  99.1 1.5 %convolution_convert_fusion = bf16[512,1024]{1,0:T(8,128)(2,1)} fusion(f32[64,1024]{1,0:T(8,128)S(1)} %add_bitcast_fusion, bf16[32,512]{1,0:T(8,128)(2,1)S(1)} %collective-permute-done.19, bf16[32,512]{1,0:T(8,128)(2,1)S(1)} %add_convert_fusion, pred[]{:T(512)S(6)} %eq.35, f32[1,64,1024]{2,1,0:T(8,128)S(1)} %copy-done.4, f32[1,64,1024]{2,1,0:T(8,128)S(1)} %copy-done.8, ...), kind=kOutput, calls=%fused_computation.7 | convolution fusion | flops 68976640 | bytes 2162689 | tf_op jit(solution)/shard_map/dot_general | solution.py:267
  100.6 7.5 %all-to-all-start.2 = ((bf16[32,16,1024]{2,1,0:T(8,128)(2,1)}), bf16[32,16,1024]{2,1,0:T(8,128)(2,1)S(1)}, u32[]{:S(2)}, u32[]{:S(2)}) async-start(bf16[32,16,1024]{2,1,0:T(8,128)(2,1)} %bitcast.54), calls=%async_computation.2 | async-start | bytes 2097152 | tf_op jit(solution)/shard_map/all_to_all | solution.py:271
  109.5 26.9 %all-to-all-done.2 = bf16[32,16,1024]{2,1,0:T(8,128)(2,1)S(1)} async-done(((bf16[32,16,1024]{2,1,0:T(8,128)(2,1)}), bf16[32,16,1024]{2,1,0:T(8,128)(2,1)S(1)}, u32[]{:S(2)}, u32[]{:S(2)}) %all-to-all-start.2) | async-done | bytes 1048608 | tf_op jit(solution)/shard_map/all_to_all | solution.py:271
  136.5 3.8 %shard_map.198 = bf16[128,1024]{1,0:T(8,128)(2,1)} custom-call(s32[128,1]{1,0:T(8,128)S(1)} %sub.37.place_ref, s32[128,1]{1,0:T(8,128)S(1)} %copy.42.length_ref, bf16[512,1024]{1,0:T(8,128)(2,1)S(1)} %bitcast.131, bf16[128,1024]{1,0:T(8,128)(2,1)S(1)} %copy-done.1, bf16[2,128,1,48,128]{4,3,2,1,0:T(8,128)(2,1)} %cache_hbm.1, bf16[2,128,128]{2,1,0:T(8,128)(2,1)S(1)} %bitcast.132), custom_call_target="tpu_custom_call" | custom-call | tf_op jit(solution)/shard_map/pallas_call | solution.py:190
  (77 shorter events, 9.6 us)
Async XLA Ops:
  0.6 12.0 %copy-start = (bf16[128,640]{1,0:T(8,128)(2,1)S(1)}, bf16[128,640]{1,0:T(8,128)(2,1)}, u32[]{:S(2)}) copy-start(bf16[128,640]{1,0:T(8,128)(2,1)} %param.26) | copy-start | bytes 491524
  0.6 13.2 %copy-start.3 = (bf16[1,32,640,64]{2,3,1,0:T(8,128)(2,1)S(1)}, bf16[1,32,640,64]{2,3,1,0:T(8,128)(2,1)}, u32[]{:S(2)}) copy-start(bf16[1,32,640,64]{2,3,1,0:T(8,128)(2,1)} %param.15) | copy-start | bytes 7864324
  1.9 12.0 %collective-permute-start = (bf16[2,64,640]{2,1,0:T(8,128)(2,1)S(1)}, bf16[2,64,640]{2,1,0:T(8,128)(2,1)S(1)}, u32[]{:S(2)}, u32[]{:S(2)}) collective-permute-start(bf16[2,64,640]{2,1,0:T(8,128)(2,1)S(1)} %get-tuple-element.70), channel_id=1, source_target_pairs={{0,32},{32,64},{64,96},{96,128},{128,160},{160,192},{192,224},{224... | collective-permute-start | bytes 491528 | tf_op jit(solution)/shard_map/ppermute | solution.py:36
  3.9 10.0 %collective-permute-start.1 = (bf16[2,64,640]{2,1,0:T(8,128)(2,1)S(1)}, bf16[2,64,640]{2,1,0:T(8,128)(2,1)S(1)}, u32[]{:S(2)}, u32[]{:S(2)}) collective-permute-start(bf16[2,64,640]{2,1,0:T(8,128)(2,1)S(1)} %get-tuple-element.71), channel_id=1, source_target_pairs={{0,224},{32,0},{64,32},{96,64},{128,96},{160,128},{192,160},{224,1... | collective-permute-start | bytes 491528 | tf_op jit(solution)/shard_map/ppermute | solution.py:36
  10.2 17.0 %collective-permute-start.4 = (bf16[4,64,1024]{2,1,0:T(8,128)(2,1)}, bf16[4,64,1024]{2,1,0:T(8,128)(2,1)}, u32[]{:S(2)}, u32[]{:S(2)}) collective-permute-start(bf16[4,64,1024]{2,1,0:T(8,128)(2,1)} %get-tuple-element.83), channel_id=1, source_target_pairs={{0,8},{8,16},{16,24},{24,0},{1,9},{9,17},{17,25},{25,1},{2,10},{10... | collective-permute-start | bytes 1572872 | tf_op jit(solution)/shard_map/ppermute | solution.py:36
  11.7 15.4 %collective-permute-start.5 = (bf16[4,64,1024]{2,1,0:T(8,128)(2,1)}, bf16[4,64,1024]{2,1,0:T(8,128)(2,1)}, u32[]{:S(2)}, u32[]{:S(2)}) collective-permute-start(bf16[4,64,1024]{2,1,0:T(8,128)(2,1)} %get-tuple-element.84), channel_id=1, source_target_pairs={{0,24},{8,0},{16,8},{24,16},{1,25},{9,1},{17,9},{25,17},{2,26},{10... | collective-permute-start | bytes 1572872 | tf_op jit(solution)/shard_map/ppermute | solution.py:36
  14.8 43.9 %all-to-all-start = ((bf16[32,16,640]{2,1,0:T(8,128)(2,1)}), bf16[32,16,640]{2,1,0:T(8,128)(2,1)S(1)}, u32[]{:S(2)}, u32[]{:S(2)}) async-start(bf16[32,16,640]{2,1,0:T(8,128)(2,1)} %bitcast.24), calls=%async_computation | async-start | bytes 1310720 | tf_op jit(solution)/shard_map/all_to_all | solution.py:247
  23.8 23.0 %collective-permute-start.2 = (bf16[4,64,640]{2,1,0:T(8,128)(2,1)}, bf16[4,64,640]{2,1,0:T(8,128)(2,1)}, u32[]{:S(2)}, u32[]{:S(2)}) collective-permute-start(bf16[4,64,640]{2,1,0:T(8,128)(2,1)} %get-tuple-element.79), channel_id=1, source_target_pairs={{0,32},{32,64},{64,96},{96,128},{128,160},{160,192},{192,224},{224... | collective-permute-start | bytes 983048 | tf_op jit(solution)/shard_map/ppermute | solution.py:36
  25.3 21.5 %collective-permute-start.3 = (bf16[4,64,640]{2,1,0:T(8,128)(2,1)}, bf16[4,64,640]{2,1,0:T(8,128)(2,1)}, u32[]{:S(2)}, u32[]{:S(2)}) collective-permute-start(bf16[4,64,640]{2,1,0:T(8,128)(2,1)} %get-tuple-element.80), channel_id=1, source_target_pairs={{0,224},{32,0},{64,32},{96,64},{128,96},{160,128},{192,160},{224,1... | collective-permute-start | bytes 983048 | tf_op jit(solution)/shard_map/ppermute | solution.py:36
  30.9 33.1 %collective-permute-start.10 = (bf16[8,64,1024]{2,1,0:T(8,128)(2,1)}, bf16[8,64,1024]{2,1,0:T(8,128)(2,1)}, u32[]{:S(2)}, u32[]{:S(2)}) collective-permute-start(bf16[8,64,1024]{2,1,0:T(8,128)(2,1)} %get-tuple-element.102), channel_id=1, source_target_pairs={{0,8},{8,16},{16,24},{24,0},{1,9},{9,17},{17,25},{25,1},{2,10},{10... | collective-permute-start | bytes 3145736 | tf_op jit(solution)/shard_map/ppermute | solution.py:36
  32.3 31.6 %collective-permute-start.11 = (bf16[8,64,1024]{2,1,0:T(8,128)(2,1)}, bf16[8,64,1024]{2,1,0:T(8,128)(2,1)}, u32[]{:S(2)}, u32[]{:S(2)}) collective-permute-start(bf16[8,64,1024]{2,1,0:T(8,128)(2,1)} %get-tuple-element.103), channel_id=1, source_target_pairs={{0,24},{8,0},{16,8},{24,16},{1,25},{9,1},{17,9},{25,17},{2,26},{10... | collective-permute-start | bytes 3145736 | tf_op jit(solution)/shard_map/ppermute | solution.py:36
  48.9 9.7 %collective-permute-start.6 = (bf16[4,64,640]{2,1,0:T(8,128)(2,1)}, bf16[4,64,640]{2,1,0:T(8,128)(2,1)}, u32[]{:S(2)}, u32[]{:S(2)}) collective-permute-start(bf16[4,64,640]{2,1,0:T(8,128)(2,1)} %get-tuple-element.92), channel_id=1, source_target_pairs={{0,32},{32,64},{64,96},{96,128},{128,160},{160,192},{192,224},{224... | collective-permute-start | bytes 983048 | tf_op jit(solution)/shard_map/ppermute | solution.py:36
  49.1 9.6 %collective-permute-start.7 = (bf16[4,64,640]{2,1,0:T(8,128)(2,1)}, bf16[4,64,640]{2,1,0:T(8,128)(2,1)}, u32[]{:S(2)}, u32[]{:S(2)}) collective-permute-start(bf16[4,64,640]{2,1,0:T(8,128)(2,1)} %get-tuple-element.93), channel_id=1, source_target_pairs={{0,224},{32,0},{64,32},{96,64},{128,96},{160,128},{192,160},{224,1... | collective-permute-start | bytes 983048 | tf_op jit(solution)/shard_map/ppermute | solution.py:36
  60.7 11.7 %collective-permute-start.8 = (bf16[4,64,640]{2,1,0:T(8,128)(2,1)}, bf16[4,64,640]{2,1,0:T(8,128)(2,1)S(1)}, u32[]{:S(2)}, u32[]{:S(2)}) collective-permute-start(bf16[4,64,640]{2,1,0:T(8,128)(2,1)} %get-tuple-element.98), channel_id=1, source_target_pairs={{0,32},{32,64},{64,96},{96,128},{128,160},{160,192},{192,224},{224... | collective-permute-start | bytes 983048 | tf_op jit(solution)/shard_map/ppermute | solution.py:36
  62.0 10.4 %collective-permute-start.9 = (bf16[4,64,640]{2,1,0:T(8,128)(2,1)}, bf16[4,64,640]{2,1,0:T(8,128)(2,1)S(1)}, u32[]{:S(2)}, u32[]{:S(2)}) collective-permute-start(bf16[4,64,640]{2,1,0:T(8,128)(2,1)} %get-tuple-element.99), channel_id=1, source_target_pairs={{0,224},{32,0},{64,32},{96,64},{128,96},{160,128},{192,160},{224,1... | collective-permute-start | bytes 983048 | tf_op jit(solution)/shard_map/ppermute | solution.py:36
  67.5 14.1 %copy-start.10 = (f32[1,640,64]{1,2,0:T(8,128)S(1)}, f32[1,640,64]{1,2,0:T(8,128)}, u32[]{:S(2)}) copy-start(f32[1,640,64]{1,2,0:T(8,128)} %param.17) | copy-start | bytes 491524
  67.5 14.1 %copy-start.11 = (f32[1,640,64]{1,2,0:T(8,128)S(1)}, f32[1,640,64]{1,2,0:T(8,128)}, u32[]{:S(2)}) copy-start(f32[1,640,64]{1,2,0:T(8,128)} %param.19) | copy-start | bytes 491524
  67.5 31.3 %all-to-all-start.1 = ((bf16[8,64,1024]{2,1,0:T(8,128)(2,1)}), bf16[8,64,1024]{2,1,0:T(8,128)(2,1)S(1)}, u32[]{:S(2)}, u32[]{:S(2)}) async-start(bf16[8,64,1024]{2,1,0:T(8,128)(2,1)} %fusion.1), calls=%async_computation.1 | async-start | bytes 2097152 | tf_op jit(solution)/shard_map/all_to_all | solution.py:88
  73.6 4.7 %collective-permute-start.12 = (bf16[64,640]{1,0:T(8,128)(2,1)S(1)}, bf16[64,640]{1,0:T(8,128)(2,1)S(1)}, u32[]{:S(2)}, u32[]{:S(2)}) collective-permute-start(bf16[64,640]{1,0:T(8,128)(2,1)S(1)} %get-tuple-element.110), channel_id=1, source_target_pairs={{0,8},{8,16},{16,24},{24,0},{1,9},{9,17},{17,25},{25,1},{2,10},{10... | collective-permute-start | bytes 245768 | tf_op jit(solution)/shard_map/ppermute | solution.py:36
  75.4 6.0 %collective-permute-start.13 = (bf16[64,640]{1,0:T(8,128)(2,1)S(1)}, bf16[64,640]{1,0:T(8,128)(2,1)S(1)}, u32[]{:S(2)}, u32[]{:S(2)}) collective-permute-start(bf16[64,640]{1,0:T(8,128)(2,1)S(1)} %get-tuple-element.111), channel_id=1, source_target_pairs={{0,16},{8,24},{16,0},{24,8},{1,17},{9,25},{17,1},{25,9},{2,18},{10... | collective-permute-start | bytes 245768 | tf_op jit(solution)/shard_map/ppermute | solution.py:36
  76.2 5.3 %collective-permute-start.14 = (bf16[64,640]{1,0:T(8,128)(2,1)S(1)}, bf16[64,640]{1,0:T(8,128)(2,1)S(1)}, u32[]{:S(2)}, u32[]{:S(2)}) collective-permute-start(bf16[64,640]{1,0:T(8,128)(2,1)S(1)} %get-tuple-element.112), channel_id=1, source_target_pairs={{0,24},{8,0},{16,8},{24,16},{1,25},{9,1},{17,9},{25,17},{2,26},{10... | collective-permute-start | bytes 245768 | tf_op jit(solution)/shard_map/ppermute | solution.py:36
  81.6 17.5 %copy-start.4 = (f32[1,64,1024]{2,1,0:T(8,128)S(1)}, f32[1,64,1024]{2,1,0:T(8,128)}, u32[]{:S(2)}) copy-start(f32[1,64,1024]{2,1,0:T(8,128)} %param.22) | copy-start | bytes 786436
  81.6 17.4 %copy-start.6 = (f32[1,64,1024]{2,1,0:T(8,128)S(1)}, f32[1,64,1024]{2,1,0:T(8,128)}, u32[]{:S(2)}) copy-start(f32[1,64,1024]{2,1,0:T(8,128)} %param.18) | copy-start | bytes 786436
  81.6 17.4 %copy-start.8 = (f32[1,64,1024]{2,1,0:T(8,128)S(1)}, f32[1,64,1024]{2,1,0:T(8,128)}, u32[]{:S(2)}) copy-start(f32[1,64,1024]{2,1,0:T(8,128)} %param.20) | copy-start | bytes 786436
  82.9 1.4 %collective-permute-start.15 = (f32[64,512]{1,0:T(8,128)S(1)}, f32[64,512]{1,0:T(8,128)S(1)}, u32[]{:S(2)}, u32[]{:S(2)}) collective-permute-start(f32[64,512]{1,0:T(8,128)S(1)} %fusion.38), channel_id=1, source_target_pairs={{0,1},{1,0},{2,3},{3,2},{4,5},{5,4},{6,7},{7,6},{8,9},{9,8},{10,11... | collective-permute-start | bytes 393224 | tf_op jit(solution)/shard_map/ppermute | solution.py:36
  85.4 8.7 %collective-permute-start.17 = (bf16[32,512]{1,0:T(8,128)(2,1)S(1)}, bf16[32,512]{1,0:T(8,128)(2,1)S(1)}, u32[]{:S(2)}, u32[]{:S(2)}) collective-permute-start(bf16[32,512]{1,0:T(8,128)(2,1)S(1)} %convert_element_type.254), channel_id=1, source_target_pairs={{0,6},{1,7},{2,0},{3,1},{4,2},{5,3},{6,4},{7,5},{8,14},{9,15},{10,... | collective-permute-start | bytes 98312 | tf_op jit(solution)/shard_map/ppermute | solution.py:41
  88.2 5.8 %collective-permute-start.18 = (bf16[32,512]{1,0:T(8,128)(2,1)S(1)}, bf16[32,512]{1,0:T(8,128)(2,1)S(1)}, u32[]{:S(2)}, u32[]{:S(2)}) collective-permute-start(bf16[32,512]{1,0:T(8,128)(2,1)S(1)} %convert_element_type.254), channel_id=1, source_target_pairs={{0,4},{1,5},{2,6},{3,7},{4,0},{5,1},{6,2},{7,3},{8,12},{9,13},{10,... | collective-permute-start | bytes 98312 | tf_op jit(solution)/shard_map/ppermute | solution.py:41
  89.0 5.0 %collective-permute-start.16 = (bf16[32,512]{1,0:T(8,128)(2,1)S(1)}, bf16[32,512]{1,0:T(8,128)(2,1)S(1)}, u32[]{:S(2)}, u32[]{:S(2)}) collective-permute-start(bf16[32,512]{1,0:T(8,128)(2,1)S(1)} %dynamic-slice_bitcast_fusion.7), channel_id=1, source_target_pairs={{0,3},{1,2},{2,5},{3,4},{4,7},{5,6},{6,1},{7,0},{8,11},{9,10},{10,... | collective-permute-start | bytes 98312 | tf_op jit(solution)/shard_map/ppermute | solution.py:41
  94.1 5.0 %collective-permute-start.19 = (bf16[32,512]{1,0:T(8,128)(2,1)S(1)}, bf16[32,512]{1,0:T(8,128)(2,1)S(1)}, u32[]{:S(2)}, u32[]{:S(2)}) collective-permute-start(bf16[32,512]{1,0:T(8,128)(2,1)S(1)} %add_convert_fusion), channel_id=1, source_target_pairs={{0,1},{1,0},{2,3},{3,2},{4,5},{5,4},{6,7},{7,6},{8,9},{9,8},{10,11... | collective-permute-start | bytes 98312 | tf_op jit(solution)/shard_map/ppermute | solution.py:36
  100.6 35.9 %copy-start.1 = (bf16[128,1024]{1,0:T(8,128)(2,1)S(1)}, bf16[128,1024]{1,0:T(8,128)(2,1)}, u32[]{:S(2)}) copy-start(bf16[128,1024]{1,0:T(8,128)(2,1)} %frozen_ref.1) | copy-start | bytes 786436
  100.6 35.9 %copy-start.2 = (bf16[2,128,1,128]{3,1,2,0:T(8,128)(2,1)S(1)}, bf16[2,128,1,128]{3,1,2,0:T(8,128)(2,1)}, u32[]{:S(2)}) copy-start(bf16[2,128,1,128]{3,1,2,0:T(8,128)(2,1)} %param.29) | copy-start | bytes 196612
  100.6 35.9 %all-to-all-start.2 = ((bf16[32,16,1024]{2,1,0:T(8,128)(2,1)}), bf16[32,16,1024]{2,1,0:T(8,128)(2,1)S(1)}, u32[]{:S(2)}, u32[]{:S(2)}) async-start(bf16[32,16,1024]{2,1,0:T(8,128)(2,1)} %bitcast.54), calls=%async_computation.2 | async-start | bytes 2097152 | tf_op jit(solution)/shard_map/all_to_all | solution.py:271
  (7 other events, 61.6 us)
